TPU v7x, 128 devices: a whole 4x4x4 slice. The times are simulated.
128 devices in a mesh: az: 8 (over z, core), rg: 16 (over y, x).
Axes of the slice: x: 4, y: 4, z: 4, core: 2. Of those that a mesh axis runs over, the one named last changes fastest.
Arguments:
- raw: bfloat16 [2, 16384, 8320], P(None, ('az', 'rg')), may hold values from -6 to 6
- range_filter: bfloat16 [2, 4096], replicated, may hold values from -0.0625 to 0.0625
- mig_offsets: int32 [32], replicated, may hold values from 0 to 96
- mig_widths: int32 [32], replicated, may hold values from 1 to 32
- mig_coefs: bfloat16 [32, 32], replicated, may hold values from -1.5 to 1.5
- az_filter: bfloat16 [2, 4096, 4096], P(None, None, 'rg'), may hold values from -0.09375 to 0.09375
- az_lengths: int32 [4096], P('rg'), may hold values from 1024 to 4096
Outputs:
- image: float32 [2, 16384, 4096], P(None, 'az', 'rg')
All inputs are finite; a program needn't handle non-finite values.
Results may differ from a plain program's by a relative error of at most 0.0041.
Values may be sent and summed in bfloat16 or wider, within the bound.
No kernel may reach another device: no remote copies, remote signals or barrier semaphores. Data moves between devices by JAX's collectives and lax.ppermute only.
A program may use at most 192 MiB of HBM per device.

v0:
```python
import math

import jax
import jax.numpy as jnp
from jax import lax
from jax.sharding import PartitionSpec as P

CHIRP = 4096
MIGBLK = 128


DFT_PRECISION = lax.Precision.HIGH


def shifted(block, axis, distance):
    devices = range(lax.axis_size(axis))
    route = [(i - distance, i) for i in devices if i - distance in devices]
    return lax.ppermute(block, axis, route)


def phase_table(rows, cols, period, sign):
    angle = jnp.arange(rows)[:, None] * jnp.arange(cols)[None, :] % period
    theta = sign * 2.0 * math.pi / period * angle.astype(jnp.float32)
    return (jnp.cos(theta), jnp.sin(theta))


def transform(real_part, imag_part, sign):
    total, width = real_part.shape
    inner = math.gcd(total, 128)
    outer = total // inner
    real_grid = real_part.reshape(inner, outer, width)
    imag_grid = imag_part.reshape(inner, outer, width)
    cos_inner, sin_inner = phase_table(inner, inner, inner, sign)
    first_real = jnp.einsum(
        "kn,nam->kam", cos_inner, real_grid, precision=DFT_PRECISION
    ) - jnp.einsum("kn,nam->kam", sin_inner, imag_grid, precision=DFT_PRECISION)
    first_imag = jnp.einsum(
        "kn,nam->kam", cos_inner, imag_grid, precision=DFT_PRECISION
    ) + jnp.einsum("kn,nam->kam", sin_inner, real_grid, precision=DFT_PRECISION)
    cos_twist, sin_twist = phase_table(inner, outer, total, sign)
    cos_twist = cos_twist[:, :, None]
    sin_twist = sin_twist[:, :, None]
    twisted_real = first_real * cos_twist - first_imag * sin_twist
    twisted_imag = first_real * sin_twist + first_imag * cos_twist
    cos_outer, sin_outer = phase_table(outer, outer, outer, sign)
    final_real = jnp.einsum(
        "jn,knm->jkm", cos_outer, twisted_real, precision=DFT_PRECISION
    ) - jnp.einsum("jn,knm->jkm", sin_outer, twisted_imag, precision=DFT_PRECISION)
    final_imag = jnp.einsum(
        "jn,knm->jkm", cos_outer, twisted_imag, precision=DFT_PRECISION
    ) + jnp.einsum("jn,knm->jkm", sin_outer, twisted_real, precision=DFT_PRECISION)
    return (final_real.reshape(total, width), final_imag.reshape(total, width))


def correlate(extended, filter_taps, keep):
    total = extended.shape[1]
    padding = jnp.zeros((2, total - filter_taps.shape[1], filter_taps.shape[2]), jnp.float32)
    kernel = jnp.concatenate([filter_taps, padding], axis=1)
    signal_real, signal_imag = transform(extended[0], extended[1], -1.0)
    kernel_real, kernel_imag = transform(kernel[0], kernel[1], 1.0)
    product_real = signal_real * kernel_real - signal_imag * kernel_imag
    product_imag = signal_real * kernel_imag + signal_imag * kernel_real
    result_real, result_imag = transform(product_real, product_imag, 1.0)
    return jnp.stack([result_real[:keep], result_imag[:keep]]) / total


def toeplitz(taps):
    length = taps.shape[0] + MIGBLK
    padded = jnp.concatenate([taps, jnp.zeros((MIGBLK + 1,), taps.dtype)])
    rows_of = jnp.tile(padded, MIGBLK)[: MIGBLK * length].reshape(MIGBLK, length)
    return rows_of.T


def compress(raw, range_filter):
    span = MIGBLK + CHIRP
    count = (raw.shape[2] - CHIRP) // MIGBLK
    rows = raw.shape[1]
    table_real = toeplitz(range_filter[0])
    table_imag = toeplitz(range_filter[1])
    table = jnp.concatenate(
        [
            jnp.concatenate([table_real, table_imag], axis=1),
            jnp.concatenate([-table_imag, table_real], axis=1),
        ],
        axis=0,
    )

    def one_block(start):
        window = lax.dynamic_slice_in_dim(raw, start, span, 2)
        stacked = jnp.concatenate([window[0], window[1]], axis=1)
        return jnp.dot(stacked, table, preferred_element_type=jnp.float32).astype(jnp.bfloat16)

    blocks = lax.map(one_block, jnp.arange(count, dtype=jnp.int32) * MIGBLK)
    blocks = blocks.reshape(count, rows, 2, MIGBLK).transpose(2, 1, 0, 3)
    return blocks.reshape(2, rows, count * MIGBLK)


def band_matrices(offsets, widths, coefs):
    count = offsets.shape[0]
    lag = (
        jnp.arange(2 * MIGBLK)[None, :, None]
        - jnp.arange(MIGBLK)[None, None, :]
        - offsets[:, None, None]
    )
    matrix = jnp.zeros((count, 2 * MIGBLK, MIGBLK), jnp.float32)
    for band in range(coefs.shape[1]):
        chosen = (lag == band) & (band < widths[:, None, None])
        matrix = matrix + jnp.where(chosen, coefs[:, band].astype(jnp.float32)[:, None, None], 0.0)
    return matrix.astype(jnp.bfloat16)


def migrate(compressed, offsets, widths, coefs):
    count = offsets.shape[0]
    rows = compressed.shape[1]
    lower = compressed[:, :, : count * MIGBLK].reshape(2, rows, count, MIGBLK)
    upper = compressed[:, :, MIGBLK : (count + 1) * MIGBLK].reshape(2, rows, count, MIGBLK)
    windows = jnp.concatenate([lower, upper], axis=3)
    matrix = band_matrices(offsets, widths, coefs)
    moved = jnp.einsum("crbi,biq->crbq", windows, matrix, preferred_element_type=jnp.float32)
    return moved.reshape(2, rows, count * MIGBLK).astype(jnp.bfloat16)


def per_device(raw, range_filter, mig_offsets, mig_widths, mig_coefs, az_filter, az_lengths):
    compressed = compress(raw, range_filter)
    rows = compressed.shape[1]
    groups = lax.axis_size("rg")
    bins = az_lengths.shape[0]
    covered = bins * groups
    widened = jnp.concatenate(
        [compressed, jnp.zeros((2, rows, bins - MIGBLK), jnp.bfloat16)], axis=2
    )
    lower = compressed[:, :, :covered].reshape(2, rows, groups, bins)
    upper = widened[:, :, bins : bins + covered].reshape(2, rows, groups, bins)[:, :, :, :MIGBLK]
    sections = jnp.concatenate([lower, upper], axis=3).reshape(2, rows, groups * (bins + MIGBLK))
    turned = lax.all_to_all(sections, "rg", split_axis=2, concat_axis=1, tiled=True)
    count = bins // MIGBLK
    first = lax.axis_index("rg") * count
    local = migrate(
        turned,
        lax.dynamic_slice_in_dim(mig_offsets, first, count, 0),
        lax.dynamic_slice_in_dim(mig_widths, first, count, 0),
        lax.dynamic_slice_in_dim(mig_coefs, first, count, 0),
    )
    pulses = local.shape[1]
    following = shifted(local, "az", -1)
    farther = shifted(local, "az", -2)
    length_mask = jnp.arange(az_filter.shape[1])[:, None] < az_lengths[None, :]
    taps = jnp.where(length_mask[None], az_filter.astype(jnp.float32), 0.0)
    extended = jnp.concatenate([local, following, farther], axis=1).astype(jnp.float32)
    image = correlate(extended, taps, pulses)
    return image


def solution(mesh):
    return jax.shard_map(
        per_device,
        mesh=mesh,
        in_specs=(P(None, ("az", "rg"), None), P(), P(), P(), P(), P(None, None, "rg"), P("rg")),
        out_specs=P(None, "az", "rg"),
        check_vma=False,
    )
```

profile of v0, /device:TPU:1, one launch (start us, length us, event | category | flops | bytes accessed | tf_op | source)
XLA Modules:
  0.0 627.8 jit_solution(9944348763351820892)
XLA Ops:
  7.3 12.7 %maximum_maximum_fusion = bf16[8448,256]{0,1:T(8,128)(2,1)} fusion(bf16[4224,128]{0,1:T(8,128)(2,1)} %bitcast.143, bf16[4224,128]{0,1:T(8,128)(2,1)S(1)} %bitcast_negate_fusion, bf16[4224,128]{0,1:T(8,128)(2,1)S(1)} %bitcast.133), kind=kLoop, calls=%fused_computation.62 | loop fusion | flops 17301504 | bytes 7569408 | tf_op jit(solution)/shard_map/concatenate | solution.py:80
  20.0 6.5 %copy.95 = bf16[8448,256]{1,0:T(8,128)(2,1)} copy(bf16[8448,256]{0,1:T(8,128)(2,1)} %maximum_maximum_fusion) | data formatting | bytes 8650752 | tf_op jit(solution)/shard_map/while | solution.py:93
  26.5 276.7 %while.10 = (s32[]{:T(128)}, bf16[33,128,256]{1,2,0:T(8,128)(2,1)S(1)}, s32[33]{0:T(128)S(1)}, bf16[2,128,8320]{2,1,0:T(8,128)(2,1)}, bf16[8448,256]{1,0:T(8,128...) while((s32[]{:T(128)}, bf16[33,128,256]{1,2,0:T(8,128)(2,1)S(1)}, s32[33]{0:T(128)S(1)}, ...), condition=%wide.region_1.2_spmd, body=%wide.region_0.1_spmd.sunk | while | flops 558006272 | bytes 11141291 | solution.py:93
  71.6 3.0 fusion.450
  79.6 3.0 fusion.450
  87.6 3.0 fusion.450
  95.7 3.0 fusion.450
  103.7 3.0 fusion.450
  111.7 3.0 fusion.450
  119.8 3.0 fusion.450
  127.8 3.0 fusion.450
  135.8 3.0 fusion.450
  143.9 3.0 fusion.450
  151.9 3.0 fusion.450
  159.9 3.0 fusion.450
  168.0 3.0 fusion.450
  176.0 3.0 fusion.450
  184.0 3.0 fusion.450
  192.1 3.0 fusion.450
  200.1 3.0 fusion.450
  208.1 3.0 fusion.450
  216.2 3.0 fusion.450
  264.4 3.0 fusion.450
  304.3 4.9 copy.98
  309.2 7.6 %all-to-all-start = ((bf16[2,128,6144]{1,0,2:T(2,128)(2,1)}), bf16[2,128,6144]{1,0,2:T(2,128)(2,1)}, u32[]{:S(2)}, u32[]{:S(2)}) async-start(bf16[2,128,6144]{1,0,2:T(2,128)(2,1)} %bitcast.17), calls=%async_computation | async-start | bytes 6291456 | tf_op jit(solution)/shard_map/all_to_all | solution.py:135
  319.5 6.3 %convert_select_fusion = f32[2,4096,256]{2,1,0:T(8,128)} fusion(bf16[2,4096,256]{2,1,0:T(8,128)(2,1)} %param.14, pred[4096,256]{1,0:T(8,128)(4,1)S(1)} %iota_compare_fusion), kind=kLoop, calls=%fused_computation.12 | loop fusion | flops 4194304 | bytes 13631488 | tf_op jit(solution)/shard_map/jit(_where)/select_n | solution.py:148
  325.9 4.3 pad_slice_fusion.1
  330.2 7.7 %fusion.39 = f32[128,48,256]{2,0,1:T(8,128)} fusion(f32[128,48,256]{2,1,0:T(8,128)S(1)} %bitcast.118), kind=kOutput, calls=%fused_computation.50 | convolution fusion | flops 1208188928 | bytes 12582912 | tf_op jit(solution)/shard_map/kn,nam->kam/dot_general | solution.py:39
  337.9 7.6 %fusion.41 = f32[128,48,256]{2,0,1:T(8,128)} fusion(f32[128,48,256]{2,1,0:T(8,128)S(1)} %bitcast.119), kind=kOutput, calls=%fused_computation.52 | convolution fusion | flops 1208188928 | bytes 12582912 | tf_op jit(solution)/shard_map/kn,nam->kam/dot_general | solution.py:34
  345.5 8.0 %fusion.37 = f32[128,48,256]{2,0,1:T(8,128)} fusion(f32[128,48,256]{2,1,0:T(8,128)S(1)} %bitcast.114), kind=kOutput, calls=%fused_computation.48 | convolution fusion | flops 1208188928 | bytes 12582912 | tf_op jit(solution)/shard_map/kn,nam->kam/dot_general | solution.py:36
  353.6 9.9 %all-to-all-done = bf16[2,128,6144]{1,0,2:T(2,128)(2,1)} async-done(((bf16[2,128,6144]{1,0,2:T(2,128)(2,1)}), bf16[2,128,6144]{1,0,2:T(2,128)(2,1)}, u32[]{:S(2)}, u32[]{:S(2)}) %all-to-all-start) | async-done | bytes 3145760 | tf_op jit(solution)/shard_map/all_to_all | solution.py:135
  363.5 4.0 copy.99
  367.5 3.4 copy.100
  378.7 3.9 copy.102
  382.7 4.1 copy.104
  386.9 5.4 fusion.66
  393.8 3.7 collective-permute-start
  397.5 11.8 %multiply_subtract_fusion.2 = (f32[128,48,256]{2,0,1:T(8,128)S(1)}, f32[128,48,256]{2,0,1:T(8,128)S(1)}) fusion(f32[128,48]{0,1:T(8,128)S(1)} %get-tuple-element.143, f32[128,48]{0,1:T(8,128)S(1)} %get-tuple-element.144, f32[128,48,256]{2,0,1:T(8,128)} %fusion.39, f32[128,48,256]{2,0,1:T(8,128)} %fusion.41, f32[128,48,256]{2,0,1:T(8,128)} %fusion.37, ...), kind=kOutput, calls=%fused_computation.19 | convolution fusion | flops 1220771840 | bytes 37797888 | tf_op jit(solution)/shard_map/kn,nam->kam/dot_general | solution.py:37
  409.5 7.8 %fusion.31 = f32[48,128,256]{2,0,1:T(8,128)} fusion(f32[128,48,256]{2,0,1:T(8,128)S(1)} %get-tuple-element.102), kind=kOutput, calls=%fused_computation.42 | convolution fusion | flops 453005568 | bytes 12582912 | tf_op jit(solution)/shard_map/jn,knm->jkm/dot_general | solution.py:51
  417.2 7.8 %fusion.33 = f32[48,128,256]{2,0,1:T(8,128)} fusion(f32[128,48,256]{2,0,1:T(8,128)S(1)} %get-tuple-element.102), kind=kOutput, calls=%fused_computation.44 | convolution fusion | flops 453005568 | bytes 12582912 | tf_op jit(solution)/shard_map/jn,knm->jkm/dot_general | solution.py:46
  425.0 7.8 %fusion.29 = f32[48,128,256]{2,0,1:T(8,128)} fusion(f32[128,48,256]{2,0,1:T(8,128)S(1)} %get-tuple-element.103), kind=kOutput, calls=%fused_computation.40 | convolution fusion | flops 453005568 | bytes 12582912 | tf_op jit(solution)/shard_map/jn,knm->jkm/dot_general | solution.py:48
  432.7 7.3 %collective-permute-done.1 = bf16[2,2048,256]{1,2,0:T(8,128)(2,1)S(1)} collective-permute-done((bf16[2,2048,256]{1,2,0:T(8,128)(2,1)S(1)}, bf16[2,2048,256]{1,2,0:T(8,128)(2,1)S(1)}, u32[]{:S(2)}, u32[]{:S(2)}) %collective-permute-start.1) | collective-permute-done | bytes 2097184 | tf_op jit(solution)/shard_map/ppermute | solution.py:18
  440.1 24.3 %collective-permute-done = bf16[2,2048,256]{1,2,0:T(8,128)(2,1)S(1)} collective-permute-done((bf16[2,2048,256]{1,2,0:T(8,128)(2,1)S(1)}, bf16[2,2048,256]{1,2,0:T(8,128)(2,1)S(1)}, u32[]{:S(2)}, u32[]{:S(2)}) %collective-permute-start) | collective-permute-done | bytes 2097184 | tf_op jit(solution)/shard_map/ppermute | solution.py:18
  465.4 3.1 fusion.441
  468.5 3.3 copy.106
  471.8 5.2 fusion.62
  477.1 5.3 fusion.64
  482.4 3.2 copy.108
  488.3 7.9 %multiply_subtract_fusion.3 = (f32[128,48,256]{2,0,1:T(8,128)S(1)}, f32[128,48,256]{2,0,1:T(8,128)S(1)}) fusion(f32[128,48]{0,1:T(8,128)S(1)} %get-tuple-element.145, f32[128,48]{0,1:T(8,128)S(1)} %get-tuple-element.146, f32[128,48,256]{2,0,1:T(8,128)} %fusion.62, f32[128,48,256]{2,0,1:T(8,128)S(1)} %copy-done.4, f32[128,48,256]{2,0,1:T(8,128)S(1)} %fusion.60, ...), kind=kOutput, calls=%fused_computation.21 | convolution fusion | flops 1220771840 | bytes 34652160 | tf_op jit(solution)/shard_map/kn,nam->kam/dot_general | solution.py:37
  496.3 8.0 %fusion.47 = f32[48,128,256]{2,0,1:T(8,128)} fusion(f32[128,48,256]{2,0,1:T(8,128)S(1)} %get-tuple-element.100), kind=kOutput, calls=%fused_computation.58 | convolution fusion | flops 453005568 | bytes 12582912 | tf_op jit(solution)/shard_map/jn,knm->jkm/dot_general | solution.py:51
  504.3 7.8 %fusion.49 = f32[48,128,256]{2,0,1:T(8,128)} fusion(f32[128,48,256]{2,0,1:T(8,128)S(1)} %get-tuple-element.100), kind=kOutput, calls=%fused_computation.60 | convolution fusion | flops 453005568 | bytes 12582912 | tf_op jit(solution)/shard_map/jn,knm->jkm/dot_general | solution.py:46
  512.1 7.7 %fusion.43 = f32[48,128,256]{2,0,1:T(8,128)} fusion(f32[128,48,256]{2,0,1:T(8,128)S(1)} %get-tuple-element.101), kind=kOutput, calls=%fused_computation.54 | convolution fusion | flops 453005568 | bytes 12582912 | tf_op jit(solution)/shard_map/jn,knm->jkm/dot_general | solution.py:49
  519.8 7.9 %fusion.45 = f32[48,128,256]{2,0,1:T(8,128)} fusion(f32[128,48,256]{2,0,1:T(8,128)S(1)} %get-tuple-element.101), kind=kOutput, calls=%fused_computation.56 | convolution fusion | flops 453005568 | bytes 12582912 | tf_op jit(solution)/shard_map/jn,knm->jkm/dot_general | solution.py:48
  527.7 23.2 %multiply_subtract_fusion.1 = (f32[48,128,256]{2,0,1:T(8,128)}, f32[48,128,256]{2,0,1:T(8,128)}) fusion(f32[48,128,256]{2,0,1:T(8,128)} %fusion.31, f32[48,128,256]{2,0,1:T(8,128)} %fusion.43, f32[48,128,256]{2,0,1:T(8,128)} %fusion.47, f32[48,128,256]{2,0,1:T(8,128)} %fusion.33, f32[48,128,256]{2,0,1:T(8,128)} %fusion.29, f32[48,128,256]{2,0,1:T(8,128)} %fusion.49, ...), kind=kOutput, calls=%fused_computation.17 | convolution fusion | flops 468734208 | bytes 62914560 | tf_op jit(solution)/shard_map/jn,knm->jkm/dot_general | solution.py:49
  550.8 6.4 %copy.124 = f32[48,128,256]{2,1,0:T(8,128)S(1)} copy(f32[48,128,256]{2,0,1:T(8,128)} %get-tuple-element.96) | data formatting | bytes 12582912 | tf_op jit(solution)/shard_map/sub | solution.py:61
  557.3 6.4 %fusion.23 = f32[128,48,256]{2,0,1:T(8,128)S(1)} fusion(f32[128,48,256]{2,1,0:T(8,128)S(1)} %bitcast.120), kind=kOutput, calls=%fused_computation.34 | convolution fusion | flops 1208188928 | bytes 12582912 | tf_op jit(solution)/shard_map/kn,nam->kam/dot_general | solution.py:39
  563.7 7.9 %fusion.25 = f32[128,48,256]{2,0,1:T(8,128)} fusion(f32[128,48,256]{2,1,0:T(8,128)S(1)} %bitcast.121), kind=kOutput, calls=%fused_computation.36 | convolution fusion | flops 1208188928 | bytes 12582912 | tf_op jit(solution)/shard_map/kn,nam->kam/dot_general | solution.py:34
  571.6 3.6 copy.126
  575.2 7.7 %fusion.21 = f32[128,48,256]{2,0,1:T(8,128)} fusion(f32[128,48,256]{2,1,0:T(8,128)S(1)} %bitcast.112), kind=kOutput, calls=%fused_computation.32 | convolution fusion | flops 1208188928 | bytes 12582912 | tf_op jit(solution)/shard_map/kn,nam->kam/dot_general | solution.py:36
  582.9 11.9 %multiply_add_fusion = (f32[128,48,256]{2,0,1:T(8,128)S(1)}, f32[128,48,256]{2,0,1:T(8,128)S(1)}) fusion(f32[128,48]{0,1:T(8,128)S(1)} %get-tuple-element.143, f32[128,48]{0,1:T(8,128)S(1)} %get-tuple-element.144, f32[128,48,256]{2,0,1:T(8,128)S(1)} %fusion.23, f32[128,48,256]{2,0,1:T(8,128)} %fusion.25, f32[128,48,256]{2,0,1:T(8,128)} %fusion.21, ...), kind=kOutput, calls=%fused_computation.14 | convolution fusion | flops 1220771840 | bytes 37797888 | tf_op jit(solution)/shard_map/kn,nam->kam/dot_general | solution.py:37
  594.8 6.7 %fusion.11 = f32[48,128,256]{2,0,1:T(8,128)S(1)} fusion(f32[128,48,256]{2,0,1:T(8,128)S(1)} %get-tuple-element.98), kind=kOutput, calls=%fused_computation.22 | convolution fusion | flops 453005568 | bytes 12582912 | tf_op jit(solution)/shard_map/jn,knm->jkm/dot_general | solution.py:49
  601.5 6.8 %fusion.13 = f32[48,128,256]{2,0,1:T(8,128)S(1)} fusion(f32[128,48,256]{2,0,1:T(8,128)S(1)} %get-tuple-element.98), kind=kOutput, calls=%fused_computation.24 | convolution fusion | flops 453005568 | bytes 12582912 | tf_op jit(solution)/shard_map/jn,knm->jkm/dot_general | solution.py:48
  608.3 6.6 %fusion.15 = f32[48,128,256]{2,0,1:T(8,128)S(1)} fusion(f32[128,48,256]{2,0,1:T(8,128)S(1)} %get-tuple-element.99), kind=kOutput, calls=%fused_computation.26 | convolution fusion | flops 453005568 | bytes 12582912 | tf_op jit(solution)/shard_map/jn,knm->jkm/dot_general | solution.py:51
  614.9 6.9 %fusion.17 = f32[48,128,256]{2,0,1:T(8,128)S(1)} fusion(f32[128,48,256]{2,0,1:T(8,128)S(1)} %get-tuple-element.99), kind=kOutput, calls=%fused_computation.28 | convolution fusion | flops 453005568 | bytes 12582912 | tf_op jit(solution)/shard_map/jn,knm->jkm/dot_general | solution.py:46
  (238 shorter events, 170.4 us)
Async XLA Ops:
  0.0 316.8 %copy-start = (bf16[32,32]{1,0:T(8,128)(2,1)S(1)}, bf16[32,32]{1,0:T(8,128)(2,1)}, u32[]{:S(2)}) copy-start(bf16[32,32]{1,0:T(8,128)(2,1)} %param.13) | copy-start | bytes 6148
  7.3 19.2 %copy-start.5 = (bf16[33,128,256]{1,2,0:T(8,128)(2,1)S(1)}, bf16[33,128,256]{1,2,0:T(8,128)(2,1)}, u32[]{:S(2)}) copy-start(bf16[33,128,256]{1,2,0:T(8,128)(2,1)} %custom-call) | copy-start | bytes 6488068
  304.2 13.9 %copy-start.17 = (s32[32]{0:T(128)S(1)}, s32[32]{0:T(128)}, u32[]{:S(2)}) copy-start(s32[32]{0:T(128)} %param.11) | copy-start | bytes 388
  304.3 14.5 %copy-start.6 = (s32[256]{0:T(256)S(1)}, s32[256]{0:T(256)}, u32[]{:S(2)}) copy-start(s32[256]{0:T(256)} %param.15) | copy-start | bytes 3076
  309.2 54.3 %all-to-all-start = ((bf16[2,128,6144]{1,0,2:T(2,128)(2,1)}), bf16[2,128,6144]{1,0,2:T(2,128)(2,1)}, u32[]{:S(2)}, u32[]{:S(2)}) async-start(bf16[2,128,6144]{1,0,2:T(2,128)(2,1)} %bitcast.17), calls=%async_computation | async-start | bytes 6291456 | tf_op jit(solution)/shard_map/all_to_all | solution.py:135
  319.5 6.3 %copy-start.7 = (s32[32]{0:T(128)S(1)}, s32[32]{0:T(128)}, u32[]{:S(2)}) copy-start(s32[32]{0:T(128)} %param.12) | copy-start | bytes 388
  330.2 15.4 %copy-start.2 = (f32[1,6144,256]{2,1,0:T(8,128)}, f32[1,6144,256]{2,1,0:T(8,128)S(1)}, u32[]{:S(2)}) copy-start(f32[1,6144,256]{2,1,0:T(8,128)S(1)} %get-tuple-element.105) | copy-start | bytes 18874372
  376.1 10.7 %copy-start.8 = (f32[2]{0:T(128)S(1)}, f32[2]{0:T(128)}, u32[]{:S(2)}) copy-start(f32[2]{0:T(128)} %get-tuple-element.73) | copy-start | bytes 28
  376.1 10.7 %copy-start.9 = (f32[2]{0:T(128)S(1)}, f32[2]{0:T(128)}, u32[]{:S(2)}) copy-start(f32[2]{0:T(128)} %get-tuple-element.74) | copy-start | bytes 28
  376.1 10.7 %copy-start.10 = (f32[2]{0:T(128)S(1)}, f32[2]{0:T(128)}, u32[]{:S(2)}) copy-start(f32[2]{0:T(128)} %get-tuple-element.75) | copy-start | bytes 28
  376.1 10.7 %copy-start.11 = (f32[2]{0:T(128)S(1)}, f32[2]{0:T(128)}, u32[]{:S(2)}) copy-start(f32[2]{0:T(128)} %get-tuple-element.76) | copy-start | bytes 28
  376.1 10.7 %copy-start.12 = (f32[2]{0:T(128)S(1)}, f32[2]{0:T(128)}, u32[]{:S(2)}) copy-start(f32[2]{0:T(128)} %get-tuple-element.77) | copy-start | bytes 28
  376.1 10.7 %copy-start.13 = (f32[2]{0:T(128)S(1)}, f32[2]{0:T(128)}, u32[]{:S(2)}) copy-start(f32[2]{0:T(128)} %get-tuple-element.78) | copy-start | bytes 28
  376.2 10.7 %copy-start.14 = (f32[2]{0:T(128)S(1)}, f32[2]{0:T(128)}, u32[]{:S(2)}) copy-start(f32[2]{0:T(128)} %get-tuple-element.79) | copy-start | bytes 28
  376.2 10.7 %copy-start.15 = (f32[2]{0:T(128)S(1)}, f32[2]{0:T(128)}, u32[]{:S(2)}) copy-start(f32[2]{0:T(128)} %get-tuple-element.80) | copy-start | bytes 28
  376.2 10.7 %copy-start.16 = (f32[2]{0:T(128)S(1)}, f32[2]{0:T(128)}, u32[]{:S(2)}) copy-start(f32[2]{0:T(128)} %get-tuple-element.81) | copy-start | bytes 28
  376.2 10.7 %copy-start.18 = (s32[2]{0:T(128)S(1)}, s32[2]{0:T(128)}, u32[]{:S(2)}) copy-start(s32[2]{0:T(128)} %dynamic_slice.16) | copy-start | bytes 28
  382.7 14.8 %slice-start = ((s8[6291456]{0:T(1024)(128)(4,1)}), s8[2097152]{0:T(1024)(128)(4,1)S(1)}, s32[]{:S(2)}) async-start(s8[6291456]{0:T(1024)(128)(4,1)} %bitcast.115), calls=%async_computation.1 | async-start | bytes 4194304
  386.8 10.7 %slice-start.1 = ((s8[6291456]{0:T(1024)(128)(4,1)}), s8[4194304]{0:T(1024)(128)(4,1)S(1)}, s32[]{:S(2)}) async-start(s8[6291456]{0:T(1024)(128)(4,1)} %bitcast.115), calls=%async_computation.2 | async-start | bytes 8388608
  392.5 47.6 %collective-permute-start.1 = (bf16[2,2048,256]{1,2,0:T(8,128)(2,1)S(1)}, bf16[2,2048,256]{1,2,0:T(8,128)(2,1)S(1)}, u32[]{:S(2)}, u32[]{:S(2)}) collective-permute-start(bf16[2,2048,256]{1,2,0:T(8,128)(2,1)S(1)} %bitcast.137), channel_id=1, source_target_pairs={{32,0},{48,16},{64,32},{80,48},{96,64},{112,80},{33,1},{49,17},{65... | collective-permute-start | bytes 6291464 | tf_op jit(solution)/shard_map/ppermute | solution.py:18
  393.8 70.6 %collective-permute-start = (bf16[2,2048,256]{1,2,0:T(8,128)(2,1)S(1)}, bf16[2,2048,256]{1,2,0:T(8,128)(2,1)S(1)}, u32[]{:S(2)}, u32[]{:S(2)}) collective-permute-start(bf16[2,2048,256]{1,2,0:T(8,128)(2,1)S(1)} %bitcast.138), channel_id=1, source_target_pairs={{16,0},{32,16},{48,32},{64,48},{80,64},{96,80},{112,96},{17,1},{33... | collective-permute-start | bytes 6291464 | tf_op jit(solution)/shard_map/ppermute | solution.py:18
  409.3 15.7 %copy-start.3 = (f32[128,48,256]{2,0,1:T(8,128)}, f32[128,48,256]{2,0,1:T(8,128)S(1)}, u32[]{:S(2)}) copy-start(f32[128,48,256]{2,0,1:T(8,128)S(1)} %get-tuple-element.103) | copy-start | bytes 18874372
  485.6 2.8 copy-start.4
  512.1 15.6 %slice-start.2 = ((s8[6291456]{0:T(1024)(128)(4,1)}), s8[4194304]{0:T(1024)(128)(4,1)S(1)}, s32[]{:S(2)}) async-start(s8[6291456]{0:T(1024)(128)(4,1)} %bitcast.122), calls=%async_computation.3 | async-start | bytes 8388608
  519.8 7.9 %slice-start.3 = ((s8[6291456]{0:T(1024)(128)(4,1)}), s8[2097152]{0:T(1024)(128)(4,1)S(1)}, s32[]{:S(2)}) async-start(s8[6291456]{0:T(1024)(128)(4,1)} %bitcast.122), calls=%async_computation.4 | async-start | bytes 4194304
  557.3 14.3 %slice-start.4 = ((s8[6291456]{0:T(1024)(128)(4,1)}), s8[4194304]{0:T(1024)(128)(4,1)S(1)}, s32[]{:S(2)}) async-start(s8[6291456]{0:T(1024)(128)(4,1)} %bitcast.128), calls=%async_computation.5 | async-start | bytes 8388608
  563.7 7.9 %slice-start.5 = ((s8[6291456]{0:T(1024)(128)(4,1)}), s8[2097152]{0:T(1024)(128)(4,1)S(1)}, s32[]{:S(2)}) async-start(s8[6291456]{0:T(1024)(128)(4,1)} %bitcast.128), calls=%async_computation.6 | async-start | bytes 4194304
  623.5 4.1 copy-start.1
where the time goes:
time: 640 us; the launch traced here: 628 us
  matrix products  298 us (47%)
  local copies, waits for them, and re-layouts  172 us (27%)
  loops' own time  77.1 us (12%)
  waiting for transfers between devices  41.6 us (6%)
  other arithmetic  25.8 us (4%)
  starting transfers between devices  12.6 us (2%)
    dot_general x33, matrix products, one_block(): jnp.dot(stacked, table, preferred_element_type=jnp.float32)  97.6 us
    squeeze x33, local copies, waits for them, and re-layouts, one_block(): stacked = jnp.concatenate([window[0], window[1]], axis=1)  78.4 us
    another operation x1, loops' own time, compress(): blocks = lax.map(one_block, jnp.arange(count, dtype=jnp.int32) * MIGBLK)  77.1 us
    dot_general x3, matrix products, transform(): jnp.einsum('jn,knm->jkm', cos_outer, twisted_imag, precision=DFT_PRECISION)  37.6 us
    ppermute x2, waiting for transfers between devices, shifted(): return lax.ppermute(block, axis, route)  31.7 us
    dot_general x3, matrix products, transform(): jnp.einsum('kn,nam->kam', cos_inner, imag_grid, precision=DFT_PRECISION)  31.6 us
    dot_general x3, matrix products, transform(): jnp.einsum('jn,knm->jkm', cos_outer, twisted_real, precision=DFT_PRECISION)  22.4 us
    dot_general x3, matrix products, transform(): jnp.einsum('jn,knm->jkm', sin_outer, twisted_imag, precision=DFT_PRECISION)  22.4 us
  transfers between devices with their start and end apart: 3, of which 3 were waited for; matrix products, arithmetic and copies ran while one was open for 11% of the time, Pallas kernels for 0%

commit v1 on v0

v1 whole, which is shorter than its diff:
```python
import functools
import math

import jax
import jax.numpy as jnp
import numpy as np
from jax import lax
from jax.experimental import pallas as pl
from jax.experimental.pallas import tpu as pltpu
from jax.sharding import PartitionSpec as P

BF = jnp.bfloat16
F32 = jnp.float32
BLK = 128
TAPB = 32
NBLK = 32
NOUT = 33
NSAMP = 65
N1 = 160
MSRC = 128
MOUT = 128
MFIL = 32
NBIN = 32
VMEM = 50 * 1024 * 1024
NT = (((1,), (1,)), ((), ()))


def dot(a, b):
    return jnp.dot(a, b, preferred_element_type=F32)


def filter_rows(range_filter):
    padded = jnp.pad(range_filter.astype(F32), ((0, 0), (BLK - 1, BLK + 1)))
    first = padded[:, : NOUT * BLK].reshape(2, NOUT, BLK)[:, :, ::-1]
    second = padded[:, BLK:].reshape(2, NOUT, BLK)[:, :, ::-1]
    return jnp.concatenate([first, second], axis=2).transpose(1, 0, 2)


def compress_kernel(off_ref, wid_ref, base_ref, coef_ref, raw_ref, out_ref, x_ref, g_ref, c_ref):
    def arrange(s, _):
        o = pl.multiple_of(s * BLK, BLK)
        x_ref[pl.ds(o, BLK), 0:BLK] = raw_ref[0, :, pl.ds(o, BLK)]
        x_ref[pl.ds(o, BLK), BLK:] = raw_ref[1, :, pl.ds(o, BLK)]
        return 0

    lax.fori_loop(0, NSAMP, arrange, 0, unroll=5)

    def table(j, _):
        o = pl.multiple_of(j * 2 * BLK, 2 * BLK)
        rows = base_ref[j]

        def spread(row):
            wide = jnp.broadcast_to(row, (BLK, 2 * BLK))
            return pltpu.roll(wide, 0, 1, stride=1, stride_axis=0)[:, :BLK]

        re = spread(rows[0:1])
        im = spread(rows[1:2])
        g_ref[pl.ds(o, BLK), 0:BLK] = re.astype(BF)
        g_ref[pl.ds(o, BLK), BLK:] = im.astype(BF)
        g_ref[pl.ds(o + BLK, BLK), 0:BLK] = (-im).astype(BF)
        g_ref[pl.ds(o + BLK, BLK), BLK:] = re.astype(BF)
        return 0

    lax.fori_loop(0, NOUT, table, 0, unroll=3)

    group = 11
    rows = group * BLK

    def multiply(g, _):
        r0 = pl.multiple_of(g * rows, BLK)
        acc = jnp.zeros((rows, 2 * BLK), F32)
        for j in range(NOUT):
            acc = acc + dot(x_ref[pl.ds(r0 + j * BLK, rows), :], g_ref[j * 2 * BLK : (j + 1) * 2 * BLK, :])
        out = acc.astype(BF)
        for b in range(group):
            part = out[b * BLK : (b + 1) * BLK]
            c_ref[g * group + b, 0:BLK, :] = part[:, :BLK]
            c_ref[g * group + b, BLK:, :] = part[:, BLK:]
        return 0

    lax.fori_loop(0, NOUT // group, multiply, 0)

    lane = lax.broadcasted_iota(jnp.int32, (1, 2 * BLK), 1)

    def migrate(b, _):
        row = jnp.where(lane < wid_ref[b], coef_ref[pl.ds(b, 1), :], 0.0)
        row = pltpu.roll(jnp.broadcast_to(row, (8, 2 * BLK)), off_ref[b], 1)[0:1]
        wide = jnp.broadcast_to(row, (BLK, 2 * BLK))
        band = pltpu.roll(wide, 0, 1, stride=1, stride_axis=0).astype(BF)
        window = jnp.concatenate([c_ref[b], c_ref[b + 1]], axis=1)
        moved = lax.dot_general(band, window, NT, preferred_element_type=F32)
        out_ref[pl.ds(pl.multiple_of(b * BLK, BLK), BLK), :] = moved.astype(BF)
        return 0

    lax.fori_loop(0, NBLK, migrate, 0, unroll=4)


def compress(raw, range_filter, offsets, widths, coefs):
    wide_coefs = jnp.pad(coefs.astype(F32), ((0, 0), (0, 2 * BLK - coefs.shape[1])))
    vmem = pl.BlockSpec(memory_space=pltpu.VMEM)
    smem = pl.BlockSpec(memory_space=pltpu.SMEM)
    return pl.pallas_call(
        compress_kernel,
        out_shape=jax.ShapeDtypeStruct((NBLK * BLK, 2 * BLK), BF),
        in_specs=[smem, smem, vmem, vmem, vmem],
        out_specs=vmem,
        scratch_shapes=[
            pltpu.VMEM((NSAMP * BLK, 2 * BLK), BF),
            pltpu.VMEM((NOUT * 2 * BLK, 2 * BLK), BF),
            pltpu.VMEM((NOUT, 2 * BLK, BLK), BF),
        ],
        compiler_params=pltpu.CompilerParams(vmem_limit_bytes=VMEM),
        cost_estimate=pl.CostEstimate(flops=18_300_000_000, bytes_accessed=8_000_000, transcendentals=0),
    )(offsets, widths, filter_rows(range_filter), wide_coefs, raw)


def split(table):
    hi = table.astype(np.float32).astype(jnp.bfloat16)
    lo = (table - hi.astype(np.float64)).astype(np.float32).astype(jnp.bfloat16)
    return hi, lo


def angles(rows, cols, period):
    return 2.0 * np.pi * (np.outer(rows, cols) % period) / period


def left_table(theta, sign):
    c, s = np.cos(theta), sign * np.sin(theta)
    return np.concatenate(split(np.block([[c, -s], [s, c]])), axis=0)


def right_table(theta, sign):
    c, s = np.cos(theta), sign * np.sin(theta)
    return np.concatenate(split(np.block([[c, s], [-s, c]])), axis=1)


def source_order(n_az, n_rg):
    s = np.arange(n_az * n_rg)
    return (s % n_az) * n_rg + s // n_az


def twiddle():
    theta = angles(np.arange(N1), np.arange(BLK), N1 * BLK)
    return np.stack([np.cos(theta), np.sin(theta)]).astype(np.float32)


def filter_kernel(taps_ref, w1_ref, tw_ref, wp_ref, h_ref):
    def pair(i, _):
        both = jnp.concatenate([taps_ref[2 * i], taps_ref[2 * i + 1]], axis=1)
        first = dot(w1_ref[...], both)
        first = first[: 2 * N1] + first[2 * N1 :]
        for u in range(2):
            re = first[:N1, u * BLK : (u + 1) * BLK]
            im = first[N1:, u * BLK : (u + 1) * BLK]
            c, s = tw_ref[0], tw_ref[1]
            turned = jnp.concatenate([re * c - im * s, im * c + re * s], axis=1)
            hi = turned.astype(BF)
            lo = (turned - hi.astype(F32)).astype(BF)
            second = dot(hi, wp_ref[...])
            third = dot(lo, wp_ref[:, : 2 * BLK])
            h_ref[2 * i + u] = (second[:, : 2 * BLK] + second[:, 2 * BLK :] + third) * (1.0 / (N1 * BLK))
        return 0

    lax.fori_loop(0, NBIN // 2, pair, 0)


def filter_spectrum(taps):
    w1 = left_table(angles(np.arange(N1), np.arange(MFIL), N1), 1.0)
    wp = right_table(angles(np.arange(BLK), np.arange(BLK), BLK), 1.0)
    vmem = pl.BlockSpec(memory_space=pltpu.VMEM)
    return pl.pallas_call(
        filter_kernel,
        out_shape=jax.ShapeDtypeStruct((NBIN, N1, 2 * BLK), F32),
        in_specs=[vmem] * 4,
        out_specs=vmem,
        compiler_params=pltpu.CompilerParams(vmem_limit_bytes=VMEM),
        cost_estimate=pl.CostEstimate(flops=4_000_000_000, bytes_accessed=8_000_000, transcendentals=0),
    )(taps, jnp.asarray(w1), jnp.asarray(twiddle()), jnp.asarray(wp))


def focus_kernel(x_ref, h_ref, w1_ref, tw_ref, wp_ref, wq_ref, w3_ref, out_ref, s_ref, z_ref):
    def widen(m, _):
        part = x_ref[m].astype(F32)
        s_ref[pl.ds(pl.multiple_of(m * NBIN, NBIN), NBIN), :] = part[:, :BLK]
        s_ref[pl.ds(pl.multiple_of((MSRC + m) * NBIN, NBIN), NBIN), :] = part[:, BLK:]
        return 0

    lax.fori_loop(0, MSRC, widen, 0, unroll=4)

    def load(b):
        return s_ref[pl.ds(b, 2 * MSRC, stride=NBIN), :].astype(BF)

    def pair(i, _):
        both = jnp.concatenate([load(2 * i), load(2 * i + 1)], axis=1)
        first = dot(w1_ref[...], both)
        first = first[: 2 * N1] + first[2 * N1 :]
        c, s = tw_ref[0], tw_ref[1]
        halves = []
        for u in range(2):
            re = first[:N1, u * BLK : (u + 1) * BLK]
            im = first[N1:, u * BLK : (u + 1) * BLK]
            halves.append(jnp.concatenate([re * c + im * s, im * c - re * s], axis=1).astype(BF))
        spectrum = dot(jnp.concatenate(halves, axis=0), wp_ref[...])
        spectrum = spectrum[:, : 2 * BLK] + spectrum[:, 2 * BLK :]
        products = []
        for u in range(2):
            xr = spectrum[u * N1 : (u + 1) * N1, :BLK]
            xi = spectrum[u * N1 : (u + 1) * N1, BLK:]
            hr = h_ref[2 * i + u, :, :BLK]
            hi = h_ref[2 * i + u, :, BLK:]
            products.append(jnp.concatenate([xr * hr - xi * hi, xr * hi + xi * hr], axis=1).astype(BF))
        back = dot(jnp.concatenate(products, axis=0), wq_ref[...])
        back = back[:, : 2 * BLK] + back[:, 2 * BLK :]
        columns = []
        for u in range(2):
            re = back[u * N1 : (u + 1) * N1, :BLK]
            im = back[u * N1 : (u + 1) * N1, BLK:]
            columns.append(jnp.concatenate([re * c - im * s, im * c + re * s], axis=0).astype(BF))
        last = dot(w3_ref[...], jnp.concatenate(columns, axis=1))
        last = last[: 2 * MOUT] + last[2 * MOUT :]
        for u in range(2):
            z_ref[pl.ds(2 * i + u, 2 * MOUT, stride=NBIN), :] = last[:, u * BLK : (u + 1) * BLK]
        return 0

    lax.fori_loop(0, NBIN // 2, pair, 0)

    n_az = out_ref.shape[0]
    rows = MOUT // n_az * NBIN

    def narrow(a, _):
        for part in range(2):
            o = pl.multiple_of((part * n_az + a) * rows, rows)
            out_ref[a, part * rows : (part + 1) * rows, :] = z_ref[pl.ds(o, rows), :].astype(BF)
        return 0

    lax.fori_loop(0, n_az, narrow, 0)


def focus(x, spectrum, n_az, n_rg):
    order = source_order(n_az, n_rg)
    w1 = left_table(angles(np.arange(N1), order, N1), -1.0)
    wp = right_table(angles(np.arange(BLK), np.arange(BLK), BLK), -1.0)
    wq = right_table(angles(np.arange(BLK), np.arange(BLK), BLK), 1.0)
    w3 = left_table(angles(np.arange(MOUT), np.arange(N1), N1), 1.0)
    vmem = pl.BlockSpec(memory_space=pltpu.VMEM)
    return pl.pallas_call(
        focus_kernel,
        out_shape=jax.ShapeDtypeStruct((n_az, 2 * MOUT // n_az * NBIN, BLK), BF),
        in_specs=[vmem] * 7,
        out_specs=vmem,
        scratch_shapes=[
            pltpu.VMEM((2 * MSRC * NBIN, BLK), F32),
            pltpu.VMEM((2 * MOUT * NBIN, BLK), F32),
        ],
        compiler_params=pltpu.CompilerParams(vmem_limit_bytes=VMEM),
        cost_estimate=pl.CostEstimate(flops=6_000_000_000, bytes_accessed=10_000_000, transcendentals=0),
    )(x, spectrum, jnp.asarray(w1), jnp.asarray(twiddle()), jnp.asarray(wp), jnp.asarray(wq), jnp.asarray(w3))


def turn_kernel(y_ref, out_ref):
    n_az, rows, _ = y_ref.shape
    for i in range(rows // NBIN):
        part = y_ref[:, i * NBIN : (i + 1) * NBIN, :].reshape(n_az * NBIN, BLK)
        out_ref[0, i * BLK : (i + 1) * BLK, :] = part.astype(F32).T


def turn(y):
    n_az, rows, _ = y.shape
    steps = 8
    return pl.pallas_call(
        turn_kernel,
        grid=(steps,),
        out_shape=jax.ShapeDtypeStruct((2, rows // NBIN // 2 * BLK, n_az * NBIN), F32),
        in_specs=[pl.BlockSpec((n_az, rows // steps, BLK), lambda g: (0, g, 0))],
        out_specs=pl.BlockSpec(
            (1, rows // NBIN // steps * BLK, n_az * NBIN), lambda g: (g // (steps // 2), g % (steps // 2), 0)
        ),
        cost_estimate=pl.CostEstimate(flops=0, bytes_accessed=6_000_000, transcendentals=0),
    )(y)


def own_taps(az_filter, az_lengths):
    first = lax.axis_index("az") * NBIN
    taps = lax.dynamic_slice_in_dim(az_filter, first, NBIN, 2)
    lengths = lax.dynamic_slice_in_dim(az_lengths, first, NBIN, 0)
    kept = jnp.arange(taps.shape[1])[:, None] < lengths[None, :]
    taps = jnp.where(kept[None], taps, jnp.zeros((), BF))
    return taps.transpose(2, 0, 1).reshape(NBIN, 2 * MFIL, BLK)


def per_device(raw, range_filter, mig_offsets, mig_widths, mig_coefs, az_filter, az_lengths):
    n_az, n_rg = lax.axis_size("az"), lax.axis_size("rg")
    moved = compress(raw, range_filter, mig_offsets, mig_widths, mig_coefs)
    moved = moved.reshape(n_rg * n_az, NBIN, 2 * BLK)
    x = lax.all_to_all(moved, ("rg", "az"), 0, 0, tiled=True)
    spectrum = filter_spectrum(own_taps(az_filter, az_lengths))
    y = focus(x, spectrum, n_az, n_rg)
    y = lax.all_to_all(y, "az", 0, 0, tiled=True)
    return turn(y)


def solution(mesh):
    return jax.shard_map(
        per_device,
        mesh=mesh,
        in_specs=(P(None, ("az", "rg"), None), P(), P(), P(), P(), P(None, None, "rg"), P("rg")),
        out_specs=P(None, "az", "rg"),
        check_vma=False,
    )
```

time: 640 us -> 138 us (0.22); the launches traced: 628 us -> 138 us
  matrix products: 298 us -> 0 us
  local copies, waits for them, and re-layouts: 172 us -> 3.98 us
  loops' own time: 77.1 us -> 0 us
  Pallas kernels: 0 us -> 73.4 us
  blocking collectives: 0 us -> 30.9 us
  waiting for transfers between devices: 41.6 us -> 11.5 us
  other arithmetic: 25.8 us -> 5.71 us
    dot_general x58 -> x0, matrix products: 298 us -> none  [the longest x33 97.6 us: one_block(): jnp.dot(stacked, table, preferred_element_type=jnp.float32)]
    squeeze x33 -> x0, local copies, waits for them, and re-layouts: 78.4 us -> none  [one_block(): stacked = jnp.concatenate([window[0], window[1]], axis=1)]
    another operation x1 -> x0, loops' own time: 77.1 us -> none  [compress(): blocks = lax.map(one_block, jnp.arange(count, dtype=jnp.int32) * MIGBLK)]
    pallas_call x0 -> x4, Pallas kernels: none -> 73.4 us  [the longest x1 29.5 us: compress(): pl.pallas_call(compress_kernel, out_shape=jax.ShapeDtypeStruct((NBLK * BL...]
    ppermute x2 -> x0, waiting for transfers between devices: 31.7 us -> none  [shifted(): return lax.ppermute(block, axis, route)]
    all_to_all x0 -> x1, blocking collectives: none -> 30.9 us  [per_device(): y = lax.all_to_all(y, 'az', 0, 0, tiled=True)]
    slice x14 -> x0, local copies, waits for them, and re-layouts: 27.1 us -> none  [the longest x3 9.57 us: correlate(): signal_real, signal_imag = transform(extended[0], extended[1], -1.0)]
    dynamic_slice x35 -> x1, local copies, waits for them, and re-layouts: 20 us -> 0.08 us  [own_taps(): lengths = lax.dynamic_slice_in_dim(az_lengths, first, NBIN, 0)]
  transfers between devices with their start and end apart: 3 -> 1, of which waited for: 3 -> 1; matrix products, arithmetic and copies ran while one was open for 11% -> 5% of each run, Pallas kernels for 0% -> 9%
where the time goes in v1:
time: 138 us
  Pallas kernels  73.4 us (53%)
  blocking collectives  30.9 us (22%)
  starting transfers between devices  12 us (9%)
  waiting for transfers between devices  11.5 us (8%)
  other arithmetic  5.71 us (4%)
  local copies, waits for them, and re-layouts  3.98 us (3%)
    all_to_all x1, blocking collectives, per_device(): y = lax.all_to_all(y, 'az', 0, 0, tiled=True)  30.9 us
    pallas_call x1, Pallas kernels, compress(): pl.pallas_call(compress_kernel, out_shape=jax.ShapeDtypeStruct((NBLK * BL...  29.5 us
    pallas_call x1, Pallas kernels, focus(): pl.pallas_call(focus_kernel, out_shape=jax.ShapeDtypeStruct((n_az, 2 * MO...  25.8 us
    all_to_all x1, starting transfers between devices, per_device(): x = lax.all_to_all(moved, ('rg', 'az'), 0, 0, tiled=True)  12 us
    pallas_call x1, Pallas kernels, filter_spectrum(): pl.pallas_call(filter_kernel, out_shape=jax.ShapeDtypeStruct((NBIN, N1, 2...  11.8 us
    all_to_all x1, waiting for transfers between devices, per_device(): x = lax.all_to_all(moved, ('rg', 'az'), 0, 0, tiled=True)  11.5 us
    pallas_call x1, Pallas kernels, turn(): pl.pallas_call(turn_kernel, grid=(steps,), out_shape=jax.ShapeDtypeStruct...  6.42 us
    select_n x1, other arithmetic, own_taps(): taps = jnp.where(kept[None], taps, jnp.zeros((), BF))  3.83 us
  transfers between devices with their start and end apart: 1, of which 1 were waited for; matrix products, arithmetic and copies ran while one was open for 5% of the time, Pallas kernels for 9%

profile of v1, /device:TPU:1, one launch (start us, length us, event | category | flops | bytes accessed | tf_op | source)
XLA Modules:
  0.0 137.6 jit_solution(17591313321493584716)
XLA Ops:
  0.0 0.7 pad_convert_fusion.1.coef_ref
  0.7 0.8 pad_convert_fusion
  1.5 0.1 rev.6
  1.7 0.1 rev.7
  1.9 0.0 copy-start
  1.9 0.6 copy-done
  2.5 0.0 copy-start.1
  2.5 0.7 copy-done.1
  3.2 29.5 %shard_map.145 = bf16[4096,256]{1,0:T(8,128)(2,1)} custom-call(s32[32]{0:T(128)S(1)} %copy-done, s32[32]{0:T(128)S(1)} %copy-done.1, f32[33,2,256]{2,1,0:T(2,128)S(1)} %maximum_bitcast_fusion.base_ref, f32[32,256]{1,0:T(8,128)S(1)} %pad_convert_fusion.1.coef_ref, bf16[2,128,8320]{2,1,0:T(8,128)(2,1)} %raw_ref.1), custom_call_target="tpu_custom_call" | custom-call | flops 18300000256 | bytes 8000000 | tf_op jit(solution)/shard_map/pallas_call | solution.py:102
  32.7 0.0 copy-start.8
  32.7 12.0 %all-to-all-start = ((bf16[128,32,256]{2,1,0:T(8,128)(2,1)}), bf16[128,32,256]{2,1,0:T(8,128)(2,1)}, u32[]{:S(2)}, u32[]{:S(2)}) async-start(bf16[128,32,256]{2,1,0:T(8,128)(2,1)} %bitcast.3), calls=%async_computation | async-start | bytes 4194304 | tf_op jit(solution)/shard_map/all_to_all | solution.py:295
  44.7 0.0 copy-done.8
  44.7 0.1 dynamic_slice.6
  44.7 0.3 iota_compare_fusion
  45.1 3.8 %dynamic-slice_select_fusion = bf16[2,4096,32]{2,1,0:T(8,128)(2,1)} fusion(bf16[2,4096,256]{2,1,0:T(8,128)(2,1)} %param.20, s32[]{:T(128)S(6)} %select_n.8, pred[4096,32]{1,0:T(8,128)(4,1)S(1)} %iota_compare_fusion), kind=kLoop, calls=%fused_computation | loop fusion | flops 262144 | bytes 1179652 | tf_op jit(solution)/shard_map/jit(_where)/select_n | solution.py:287
  48.9 0.0 copy-start.4
  48.9 0.0 copy-start.6
  48.9 0.0 copy-start.7
  48.9 2.3 %copy.17.taps_ref = bf16[32,64,128]{2,1,0:T(8,128)(2,1)S(1)} copy(bf16[32,64,128]{0,2,1:T(8,128)(2,1)} %bitcast.10) | data formatting | bytes 1048576 | tf_op jit(solution)/shard_map/reshape | solution.py:288
  51.2 0.0 copy-done.4
  51.2 0.0 copy-done.6
  51.2 0.0 copy-done.7
  51.2 0.0 copy-start.2
  51.2 0.0 copy-start.3
  51.3 0.0 copy-start.5
  51.3 11.8 %shard_map.146.h_ref = f32[32,160,256]{2,1,0:T(8,128)} custom-call(bf16[32,64,128]{2,1,0:T(8,128)(2,1)S(1)} %copy.17.taps_ref, bf16[640,64]{1,0:T(8,128)(2,1)S(1)} %copy-done.7, f32[2,160,128]{2,1,0:T(8,128)S(1)} %copy-done.6, bf16[256,512]{1,0:T(8,128)(2,1)S(1)} %copy-done.4), custom_call_target="tpu_custom_call" | custom-call | flops 4000000000 | bytes 8000000 | tf_op jit(solution)/shard_map/pallas_call | solution.py:171
  63.0 11.5 %all-to-all-done.x_ref = bf16[128,32,256]{2,1,0:T(8,128)(2,1)} async-done(((bf16[128,32,256]{2,1,0:T(8,128)(2,1)}), bf16[128,32,256]{2,1,0:T(8,128)(2,1)}, u32[]{:S(2)}, u32[]{:S(2)}) %all-to-all-start) | async-done | bytes 2097184 | tf_op jit(solution)/shard_map/all_to_all | solution.py:295
  74.5 0.0 copy-done.2
  74.5 0.0 copy-done.3
  74.5 0.0 copy-done.5
  74.5 25.8 %shard_map.147 = bf16[8,1024,128]{2,1,0:T(8,128)(2,1)S(1)} custom-call(bf16[128,32,256]{2,1,0:T(8,128)(2,1)} %all-to-all-done.x_ref, f32[32,160,256]{2,1,0:T(8,128)} %shard_map.146.h_ref, bf16[640,256]{1,0:T(8,128)(2,1)S(1)} %copy-done.3, f32[2,160,128]{2,1,0:T(8,128)S(1)} %copy-done.6, bf16[256,512]{1,0:T(8,128)(2,1)S(1)} %copy-done.5, ...), custom_call_target="tpu_custom_call" | custom-call | flops 6000000000 | bytes 10000000 | tf_op jit(solution)/shard_map/pallas_call | solution.py:246
  100.3 30.9 %all_to_all.10.y_ref = bf16[8,1024,128]{2,1,0:T(8,128)(2,1)} all-to-all(bf16[8,1024,128]{2,1,0:T(8,128)(2,1)S(1)} %shard_map.147), channel_id=1, replica_groups=mesh['az'=8,'rg'=16] {'az'}, dimensions={0} | all-to-all | bytes 4194304 | tf_op jit(solution)/shard_map/all_to_all | solution.py:298
  131.2 6.4 %shard_map.148 = f32[2,2048,256]{2,1,0:T(8,128)} custom-call(bf16[8,1024,128]{2,1,0:T(8,128)(2,1)} %all_to_all.10.y_ref), custom_call_target="tpu_custom_call" | custom-call | bytes 6000000 | tf_op jit(solution)/shard_map/pallas_call | solution.py:270
  (2 shorter events, 0.1 us)
Async XLA Ops:
  1.9 0.7 copy-start
  2.5 0.7 copy-start.1
  32.7 12.0 %copy-start.8 = (s32[256]{0:T(256)S(1)}, s32[256]{0:T(256)}, u32[]{:S(2)}) copy-start(s32[256]{0:T(256)} %param.21) | copy-start | bytes 3076
  32.7 41.8 %all-to-all-start = ((bf16[128,32,256]{2,1,0:T(8,128)(2,1)}), bf16[128,32,256]{2,1,0:T(8,128)(2,1)}, u32[]{:S(2)}, u32[]{:S(2)}) async-start(bf16[128,32,256]{2,1,0:T(8,128)(2,1)} %bitcast.3), calls=%async_computation | async-start | bytes 4194304 | tf_op jit(solution)/shard_map/all_to_all | solution.py:295
  48.9 2.3 %copy-start.4 = (bf16[256,512]{1,0:T(8,128)(2,1)S(1)}, bf16[256,512]{1,0:T(8,128)(2,1)}, u32[]{:S(2)}) copy-start(bf16[256,512]{1,0:T(8,128)(2,1)} %constant.30.clone.wp_ref.wq_ref) | copy-start | bytes 786436
  48.9 2.3 %copy-start.6 = (f32[2,160,128]{2,1,0:T(8,128)S(1)}, f32[2,160,128]{2,1,0:T(8,128)}, u32[]{:S(2)}) copy-start(f32[2,160,128]{2,1,0:T(8,128)} %constant.29.clone.tw_ref) | copy-start | bytes 491524
  48.9 2.3 %copy-start.7 = (bf16[640,64]{1,0:T(8,128)(2,1)S(1)}, bf16[640,64]{1,0:T(8,128)(2,1)}, u32[]{:S(2)}) copy-start(bf16[640,64]{1,0:T(8,128)(2,1)} %constant.28.clone.w1_ref) | copy-start | bytes 245764
  51.2 23.3 %copy-start.2 = (bf16[512,320]{1,0:T(8,128)(2,1)S(1)}, bf16[512,320]{1,0:T(8,128)(2,1)}, u32[]{:S(2)}) copy-start(bf16[512,320]{1,0:T(8,128)(2,1)} %constant.33.clone.w3_ref) | copy-start | bytes 983044
  51.2 23.3 %copy-start.3 = (bf16[640,256]{1,0:T(8,128)(2,1)S(1)}, bf16[640,256]{1,0:T(8,128)(2,1)}, u32[]{:S(2)}) copy-start(bf16[640,256]{1,0:T(8,128)(2,1)} %constant.31.clone.w1_ref) | copy-start | bytes 983044
  51.3 23.3 %copy-start.5 = (bf16[256,512]{1,0:T(8,128)(2,1)S(1)}, bf16[256,512]{1,0:T(8,128)(2,1)}, u32[]{:S(2)}) copy-start(bf16[256,512]{1,0:T(8,128)(2,1)} %constant.32.clone.wp_ref) | copy-start | bytes 786436

commit v2 on v1

v2 whole, which is shorter than its diff:
```python
import functools
import math

import jax
import jax.numpy as jnp
import numpy as np
from jax import lax
from jax.experimental import pallas as pl
from jax.experimental.pallas import tpu as pltpu
from jax.sharding import PartitionSpec as P

BF = jnp.bfloat16
F32 = jnp.float32
BLK = 128
TAPB = 32
NBLK = 32
NOUT = 33
NSAMP = 65
N1 = 160
MSRC = 128
MOUT = 128
MFIL = 32
NBIN = 32
VMEM = 60 * 1024 * 1024
GROUPS = (11, 11, 11)
EARLY = 8
NT = (((1,), (1,)), ((), ()))


def dot(a, b):
    return jnp.dot(a, b, preferred_element_type=F32)


def compress_kernel(
    off_hbm, wid_hbm, filt_ref, coef_ref, raw_hbm, out_ref, x_ref, g_ref, c_ref, f_ref, r_ref, w_ref, off_ref, wid_ref, sems, small
):
    def block_copy(s):
        o = pl.multiple_of(s * BLK, BLK)
        return pltpu.make_async_copy(raw_hbm.at[:, :, pl.ds(o, BLK)], x_ref.at[:, pl.ds(o, BLK), :], sems.at[s])

    copies = [
        pltpu.make_async_copy(off_hbm, off_ref, small.at[0]),
        pltpu.make_async_copy(wid_hbm, wid_ref, small.at[1]),
    ]

    def start(s, _):
        block_copy(s).start()
        return 0

    lax.fori_loop(0, NSAMP, start, 0)
    for copy in copies:
        copy.start()

    filt = filt_ref[...].astype(F32)
    for j in range(TAPB):
        for part in range(2):
            f_ref[part, j : j + 1, :] = filt[part : part + 1, j * BLK : (j + 1) * BLK]
    row_of = lax.broadcasted_iota(jnp.int32, (BLK, BLK), 0)
    col_of = lax.broadcasted_iota(jnp.int32, (BLK, BLK), 1)
    exchange = jnp.where(row_of + col_of == BLK - 1, 1.0, 0.0).astype(BF)
    r_ref[...] = jnp.zeros_like(r_ref)
    for part in range(2):
        r_ref[part, 1 : 1 + TAPB, :] = dot(f_ref[part].astype(BF), exchange)

    def table(j):
        o = j * 2 * BLK

        def spread(part):
            row = jnp.concatenate([r_ref[part, j + 1 : j + 2, :], r_ref[part, j : j + 1, :]], axis=1)
            wide = jnp.broadcast_to(row, (BLK, 2 * BLK))
            return pltpu.roll(wide, BLK + 1, 1, stride=1, stride_axis=0)[:, :BLK]

        re = spread(0)
        im = spread(1)
        g_ref[o : o + BLK, 0:BLK] = re.astype(BF)
        g_ref[o : o + BLK, BLK:] = im.astype(BF)
        g_ref[o + BLK : o + 2 * BLK, 0:BLK] = (-im).astype(BF)
        g_ref[o + BLK : o + 2 * BLK, BLK:] = re.astype(BF)

    def finish(s, _):
        block_copy(s).wait()
        return 0

    lane = lax.broadcasted_iota(jnp.int32, (1, BLK), 1)

    def migrate(b):
        row = jnp.where(lane < wid_ref[b], w_ref[b : b + 1, :], 0.0)
        row = jnp.concatenate([row, jnp.zeros_like(row)], axis=1)
        row = pltpu.roll(jnp.broadcast_to(row, (8, 2 * BLK)), off_ref[b], 1)[0:1]
        wide = jnp.broadcast_to(row, (BLK, 2 * BLK))
        band = pltpu.roll(wide, 0, 1, stride=1, stride_axis=0).astype(BF)
        window = jnp.concatenate([c_ref[b], c_ref[b + 1]], axis=1)
        moved = lax.dot_general(band, window, NT, preferred_element_type=F32)
        out_ref[b * BLK : (b + 1) * BLK, :] = moved.astype(BF)

    w_ref[:, 0 : coef_ref.shape[1]] = coef_ref[...].astype(F32)
    for copy in copies:
        copy.wait()
    for j in range(EARLY):
        table(j)
    lax.fori_loop(0, NSAMP, finish, 0)

    done, moved = 0, 0
    for count in GROUPS:
        rows = count * BLK
        acc = jnp.zeros((rows, 2 * BLK), F32)
        for j in range(NOUT):
            r0 = (done + j) * BLK
            both = jnp.concatenate([x_ref[0, r0 : r0 + rows, :], x_ref[1, r0 : r0 + rows, :]], axis=1)
            acc = acc + dot(both, g_ref[j * 2 * BLK : (j + 1) * 2 * BLK, :])
            if done == 0 and j + EARLY < NOUT:
                table(j + EARLY)
            if j % 2 == 1 and moved < done - 1:
                migrate(moved)
                moved += 1
        out = acc.astype(BF)
        for b in range(count):
            part = out[b * BLK : (b + 1) * BLK]
            c_ref[done + b, 0:BLK, :] = part[:, :BLK]
            c_ref[done + b, BLK:, :] = part[:, BLK:]
        done += count
    for b in range(moved, NBLK):
        migrate(b)


def compress(raw, range_filter, offsets, widths, coefs):
    vmem = pl.BlockSpec(memory_space=pltpu.VMEM)
    hbm = pl.BlockSpec(memory_space=pltpu.HBM)
    return pl.pallas_call(
        compress_kernel,
        out_shape=jax.ShapeDtypeStruct((NBLK * BLK, 2 * BLK), BF),
        in_specs=[hbm, hbm, vmem, vmem, hbm],
        out_specs=vmem,
        scratch_shapes=[
            pltpu.VMEM((2, NSAMP * BLK, BLK), BF),
            pltpu.VMEM((NOUT * 2 * BLK, 2 * BLK), BF),
            pltpu.VMEM((NOUT, 2 * BLK, BLK), BF),
            pltpu.VMEM((2, TAPB, BLK), F32),
            pltpu.VMEM((2, TAPB + 8, BLK), F32),
            pltpu.VMEM((NBLK, BLK), F32),
            pltpu.SMEM((NBLK,), jnp.int32),
            pltpu.SMEM((NBLK,), jnp.int32),
            pltpu.SemaphoreType.DMA((NSAMP,)),
            pltpu.SemaphoreType.DMA((2,)),
        ],
        compiler_params=pltpu.CompilerParams(vmem_limit_bytes=VMEM),
        cost_estimate=pl.CostEstimate(flops=18_300_000_000, bytes_accessed=8_000_000, transcendentals=0),
    )(offsets, widths, range_filter, coefs, raw)


def split(table):
    hi = table.astype(np.float32).astype(jnp.bfloat16)
    lo = (table - hi.astype(np.float64)).astype(np.float32).astype(jnp.bfloat16)
    return hi, lo


def angles(rows, cols, period):
    return 2.0 * np.pi * (np.outer(rows, cols) % period) / period


def complex_table(theta, sign):
    c, s = np.cos(theta), sign * np.sin(theta)
    return split(np.block([[c, -s], [s, c]]))


def stacked_table(theta, sign):
    return np.concatenate(complex_table(theta, sign), axis=0)


def left_table(theta, sign):
    hi, lo = complex_table(theta, sign)
    return np.concatenate([hi, hi, lo], axis=1)


def right_table(theta, sign):
    hi, lo = complex_table(theta, sign)
    return np.concatenate([hi.T, hi.T, lo.T], axis=0)


def parts(value):
    hi = value.astype(BF)
    return hi, (value - hi.astype(F32)).astype(BF)


def source_order(n_az, n_rg):
    s = np.arange(n_az * n_rg)
    return (s % n_az) * n_rg + s // n_az


def twiddle():
    theta = angles(np.arange(N1), np.arange(BLK), N1 * BLK)
    return np.stack([np.cos(theta), np.sin(theta)]).astype(np.float32)


def filter_kernel(taps_ref, w1_ref, tw_ref, wp_ref, h_ref):
    def pair(i, _):
        both = jnp.concatenate([taps_ref[2 * i], taps_ref[2 * i + 1]], axis=1)
        first = dot(w1_ref[...], both)
        first = first[: 2 * N1] + first[2 * N1 :]
        for u in range(2):
            re = first[:N1, u * BLK : (u + 1) * BLK]
            im = first[N1:, u * BLK : (u + 1) * BLK]
            c, s = tw_ref[0], tw_ref[1]
            hi, lo = parts(jnp.concatenate([re * c - im * s, im * c + re * s], axis=1))
            second = dot(jnp.concatenate([hi, lo, hi], axis=1), wp_ref[...])
            h_ref[2 * i + u] = second * (1.0 / (N1 * BLK))
        return 0

    lax.fori_loop(0, NBIN // 2, pair, 0)


def filter_spectrum(taps):
    w1 = stacked_table(angles(np.arange(N1), np.arange(MFIL), N1), 1.0)
    wp = right_table(angles(np.arange(BLK), np.arange(BLK), BLK), 1.0)
    vmem = pl.BlockSpec(memory_space=pltpu.VMEM)
    return pl.pallas_call(
        filter_kernel,
        out_shape=jax.ShapeDtypeStruct((NBIN, N1, 2 * BLK), F32),
        in_specs=[vmem] * 4,
        out_specs=vmem,
        compiler_params=pltpu.CompilerParams(vmem_limit_bytes=VMEM),
        cost_estimate=pl.CostEstimate(flops=4_000_000_000, bytes_accessed=8_000_000, transcendentals=0),
    )(taps, jnp.asarray(w1), jnp.asarray(twiddle()), jnp.asarray(wp))


def focus_kernel(x_ref, h_hbm, w1_ref, tw_ref, wp_ref, wq_ref, w3_ref, out_ref, s_ref, z_ref, h_ref, *scratch):
    stage1, stage2, stage3, sem = scratch[0:2], scratch[2:4], scratch[4:6], scratch[6]
    copy = pltpu.make_async_copy(h_hbm, h_ref, sem)
    copy.start()

    def widen(m, _):
        part = x_ref[m].astype(F32)
        s_ref[pl.ds(pl.multiple_of(m * NBIN, NBIN), NBIN), :] = part[:, :BLK]
        s_ref[pl.ds(pl.multiple_of((MSRC + m) * NBIN, NBIN), NBIN), :] = part[:, BLK:]
        return 0

    lax.fori_loop(0, MSRC, widen, 0, unroll=8)
    copy.wait()

    def load(b):
        return s_ref[pl.ds(b, 2 * MSRC, stride=NBIN), :].astype(BF)

    def coarse(i, to):
        both = jnp.concatenate([load(2 * i), load(2 * i + 1)], axis=1)
        first = dot(w1_ref[...], both)
        first = first[: 2 * N1] + first[2 * N1 :]
        c, s = tw_ref[0], tw_ref[1]
        for u in range(2):
            rows = slice(u * N1, (u + 1) * N1)
            re = first[:N1, u * BLK : (u + 1) * BLK]
            im = first[N1:, u * BLK : (u + 1) * BLK]
            to[rows, 0:BLK], to[rows, 2 * BLK : 3 * BLK] = parts(re * c + im * s)
            to[rows, BLK : 2 * BLK], to[rows, 3 * BLK :] = parts(im * c - re * s)

    def wide(at):
        return jnp.concatenate([at[...], at[:, : 2 * BLK]], axis=1)

    def fine(i, at, to):
        spectrum = dot(wide(at), wp_ref[...])
        for u in range(2):
            rows = slice(u * N1, (u + 1) * N1)
            xr = spectrum[rows, :BLK]
            xi = spectrum[rows, BLK:]
            hr = h_ref[2 * i + u, :, :BLK]
            hi = h_ref[2 * i + u, :, BLK:]
            to[rows, 0:BLK], to[rows, 2 * BLK : 3 * BLK] = parts(xr * hr - xi * hi)
            to[rows, BLK : 2 * BLK], to[rows, 3 * BLK :] = parts(xr * hi + xi * hr)

    def fine_back(at, to):
        back = dot(wide(at), wq_ref[...])
        c, s = tw_ref[0], tw_ref[1]
        for u in range(2):
            lanes = slice(u * BLK, (u + 1) * BLK)
            re = back[u * N1 : (u + 1) * N1, :BLK]
            im = back[u * N1 : (u + 1) * N1, BLK:]
            to[0:N1, lanes], to[2 * N1 : 3 * N1, lanes] = parts(re * c - im * s)
            to[N1 : 2 * N1, lanes], to[3 * N1 :, lanes] = parts(im * c + re * s)

    def coarse_back(i, at):
        last = dot(w3_ref[...], jnp.concatenate([at[...], at[: 2 * N1, :]], axis=0))
        for u in range(2):
            z_ref[pl.ds(2 * i + u, 2 * MOUT, stride=NBIN), :] = last[:, u * BLK : (u + 1) * BLK]

    pairs = NBIN // 2

    def step(q, parity, first, last):
        if first <= 3 <= last:
            coarse_back(q - 3, stage3[1 - parity])
        if first <= 2 <= last:
            fine_back(stage2[parity], stage3[parity])
        if first <= 1 <= last:
            fine(q - 1, stage1[1 - parity], stage2[1 - parity])
        if first <= 0 <= last:
            coarse(q, stage1[parity])

    for q in range(3):
        step(q, q % 2, 0, q)

    def two(i, _):
        step(3 + 2 * i, 1, 0, 3)
        step(4 + 2 * i, 0, 0, 3)
        return 0

    lax.fori_loop(0, (pairs - 4) // 2, two, 0)
    step(pairs - 1, (pairs - 1) % 2, 0, 3)
    for q in range(pairs, pairs + 3):
        step(q, q % 2, q - pairs + 1, 3)

    n_az = out_ref.shape[0]
    rows = MOUT // n_az * NBIN

    def narrow(a, _):
        for part in range(2):
            o = pl.multiple_of((part * n_az + a) * rows, rows)
            out_ref[a, part * rows : (part + 1) * rows, :] = z_ref[pl.ds(o, rows), :].astype(BF)
        return 0

    lax.fori_loop(0, n_az, narrow, 0)


def focus(x, spectrum, n_az, n_rg):
    order = source_order(n_az, n_rg)
    w1 = stacked_table(angles(np.arange(N1), order, N1), -1.0)
    wp = right_table(angles(np.arange(BLK), np.arange(BLK), BLK), -1.0)
    wq = right_table(angles(np.arange(BLK), np.arange(BLK), BLK), 1.0)
    w3 = left_table(angles(np.arange(MOUT), np.arange(N1), N1), 1.0)
    vmem = pl.BlockSpec(memory_space=pltpu.VMEM)
    return pl.pallas_call(
        focus_kernel,
        out_shape=jax.ShapeDtypeStruct((n_az, 2 * MOUT // n_az * NBIN, BLK), BF),
        in_specs=[vmem, pl.BlockSpec(memory_space=pl.ANY)] + [vmem] * 5,
        out_specs=vmem,
        scratch_shapes=[
            pltpu.VMEM((2 * MSRC * NBIN, BLK), F32),
            pltpu.VMEM((2 * MOUT * NBIN, BLK), F32),
            pltpu.VMEM((NBIN, N1, 2 * BLK), F32),
            *[pltpu.VMEM((2 * N1, 4 * BLK), BF)] * 4,
            *[pltpu.VMEM((4 * N1, 2 * BLK), BF)] * 2,
            pltpu.SemaphoreType.DMA(()),
        ],
        compiler_params=pltpu.CompilerParams(vmem_limit_bytes=VMEM),
        cost_estimate=pl.CostEstimate(flops=6_000_000_000, bytes_accessed=10_000_000, transcendentals=0),
    )(x, spectrum, jnp.asarray(w1), jnp.asarray(twiddle()), jnp.asarray(wp), jnp.asarray(wq), jnp.asarray(w3))


def turn_kernel(y_ref, out_ref):
    n_az, rows, _ = y_ref.shape
    row_of = lax.broadcasted_iota(jnp.int32, (BLK, BLK), 0)
    col_of = lax.broadcasted_iota(jnp.int32, (BLK, BLK), 1)
    unit = jnp.where(row_of == col_of, 1.0, 0.0).astype(BF)
    for i in range(rows // NBIN):
        part = y_ref[:, i * NBIN : (i + 1) * NBIN, :].reshape(n_az * NBIN, BLK)
        out_ref[0, i * BLK : (i + 1) * BLK, :] = lax.dot_general(unit, part, NT, preferred_element_type=F32)


def turn(y):
    n_az, rows, _ = y.shape
    steps = 2
    return pl.pallas_call(
        turn_kernel,
        grid=(steps,),
        out_shape=jax.ShapeDtypeStruct((2, rows // NBIN // 2 * BLK, n_az * NBIN), F32),
        in_specs=[pl.BlockSpec((n_az, rows // steps, BLK), lambda g: (0, g, 0))],
        out_specs=pl.BlockSpec(
            (1, rows // NBIN // steps * BLK, n_az * NBIN), lambda g: (g // (steps // 2), g % (steps // 2), 0)
        ),
        compiler_params=pltpu.CompilerParams(vmem_limit_bytes=VMEM),
        cost_estimate=pl.CostEstimate(flops=0, bytes_accessed=6_000_000, transcendentals=0),
    )(y)


def own_taps(az_filter, az_lengths):
    first = lax.axis_index("az") * NBIN
    taps = lax.dynamic_slice_in_dim(az_filter, first, NBIN, 2)
    lengths = lax.dynamic_slice_in_dim(az_lengths, first, NBIN, 0)
    kept = jnp.arange(taps.shape[1])[:, None] < lengths[None, :]
    taps = jnp.where(kept[None], taps, jnp.zeros((), BF))
    return taps.transpose(2, 0, 1).reshape(NBIN, 2 * MFIL, BLK)


def per_device(raw, range_filter, mig_offsets, mig_widths, mig_coefs, az_filter, az_lengths):
    n_az, n_rg = lax.axis_size("az"), lax.axis_size("rg")
    moved = compress(raw, range_filter, mig_offsets, mig_widths, mig_coefs)
    moved = moved.reshape(n_rg * n_az, NBIN, 2 * BLK)
    x = lax.all_to_all(moved, ("rg", "az"), 0, 0, tiled=True)
    spectrum = filter_spectrum(own_taps(az_filter, az_lengths))
    y = focus(x, spectrum, n_az, n_rg)
    y = lax.all_to_all(y, "az", 0, 0, tiled=True)
    return turn(y)


def solution(mesh):
    return jax.shard_map(
        per_device,
        mesh=mesh,
        in_specs=(P(None, ("az", "rg"), None), P(), P(), P(), P(), P(None, None, "rg"), P("rg")),
        out_specs=P(None, "az", "rg"),
        check_vma=False,
    )
```

time: 138 us -> 125 us (0.906)
  Pallas kernels: 73.4 us -> 63.9 us
  other arithmetic: 5.71 us -> 2.85 us
  local copies, waits for them, and re-layouts: 3.98 us -> 1.88 us
    pallas_call x1, Pallas kernels: 25.8 us -> 20.9 us  [focus(): pl.pallas_call(focus_kernel, out_shape=jax.ShapeDtypeStruct((n_az, 2 * MO...]
    pallas_call x1, Pallas kernels: 29.5 us -> 26.2 us  [compress(): pl.pallas_call(compress_kernel, out_shape=jax.ShapeDtypeStruct((NBLK * BL...]
    pallas_call x1, Pallas kernels: 6.42 us -> 3.67 us  [turn(): pl.pallas_call(turn_kernel, grid=(steps,), out_shape=jax.ShapeDtypeStruct...]
    pad x2 -> x0, other arithmetic: 1.51 us -> none  [the longest x1 0.8 us: filter_rows(): padded = jnp.pad(range_filter.astype(F32), ((0, 0), (BLK - 1, BLK + 1)))]
    pallas_call x1, Pallas kernels: 11.8 us -> 13.2 us  [filter_spectrum(): pl.pallas_call(filter_kernel, out_shape=jax.ShapeDtypeStruct((NBIN, N1, 2...]
  transfers between devices with their start and end apart: 1 -> 1, of which waited for: 1 -> 1; matrix products, arithmetic and copies ran while one was open for 5% -> 4% of each run, Pallas kernels for 9% -> 11%
where the time goes in v2:
time: 125 us
  Pallas kernels  63.9 us (51%)
  blocking collectives  32.1 us (26%)
  starting transfers between devices  12 us (10%)
  waiting for transfers between devices  12 us (10%)
  other arithmetic  2.85 us (2%)
  local copies, waits for them, and re-layouts  1.88 us (2%)
    all_to_all x1, blocking collectives, per_device(): y = lax.all_to_all(y, 'az', 0, 0, tiled=True)  32.1 us
    pallas_call x1, Pallas kernels, compress(): pl.pallas_call(compress_kernel, out_shape=jax.ShapeDtypeStruct((NBLK * BL...  26.2 us
    pallas_call x1, Pallas kernels, focus(): pl.pallas_call(focus_kernel, out_shape=jax.ShapeDtypeStruct((n_az, 2 * MO...  20.9 us
    pallas_call x1, Pallas kernels, filter_spectrum(): pl.pallas_call(filter_kernel, out_shape=jax.ShapeDtypeStruct((NBIN, N1, 2...  13.2 us
    all_to_all x1, waiting for transfers between devices, per_device(): x = lax.all_to_all(moved, ('rg', 'az'), 0, 0, tiled=True)  12 us
    all_to_all x1, starting transfers between devices, per_device(): x = lax.all_to_all(moved, ('rg', 'az'), 0, 0, tiled=True)  12 us
    pallas_call x1, Pallas kernels, turn(): pl.pallas_call(turn_kernel, grid=(steps,), out_shape=jax.ShapeDtypeStruct...  3.67 us
    select_n x1, other arithmetic, own_taps(): taps = jnp.where(kept[None], taps, jnp.zeros((), BF))  2.5 us
  transfers between devices with their start and end apart: 1, of which 1 were waited for; matrix products, arithmetic and copies ran while one was open for 4% of the time, Pallas kernels for 11%

profile of v2, /device:TPU:1, one launch (start us, length us, event | category | flops | bytes accessed | tf_op | source)
XLA Modules:
  0.0 124.7 jit_solution(8128371244068121693)
XLA Ops:
  0.0 26.2 %shard_map.145 = bf16[4096,256]{1,0:T(8,128)(2,1)} custom-call(s32[32]{0:T(128)} %off_hbm.1, s32[32]{0:T(128)} %wid_hbm.1, bf16[2,4096]{1,0:T(2,128)(2,1)} %filt_ref.1, bf16[32,32]{1,0:T(8,128)(2,1)} %coef_ref.1, bf16[2,128,8320]{2,1,0:T(8,128)(2,1)} %raw_hbm.1), custom_call_target="tpu_custom_call" | custom-call | flops 18300000256 | bytes 8000000 | tf_op jit(solution)/shard_map/pallas_call | solution.py:129
  26.2 0.0 copy-start
  26.2 12.0 %all-to-all-start = ((bf16[128,32,256]{2,1,0:T(8,128)(2,1)}), bf16[128,32,256]{2,1,0:T(8,128)(2,1)}, u32[]{:S(2)}, u32[]{:S(2)}) async-start(bf16[128,32,256]{2,1,0:T(8,128)(2,1)} %bitcast.5), calls=%async_computation | async-start | bytes 4194304 | tf_op jit(solution)/shard_map/all_to_all | solution.py:385
  38.2 0.0 copy-done
  38.2 0.1 dynamic_slice.6
  38.3 0.3 iota_compare_fusion
  38.6 2.5 %dynamic-slice_select_fusion = bf16[2,4096,32]{2,1,0:T(8,128)(2,1)S(1)} fusion(bf16[2,4096,256]{2,1,0:T(8,128)(2,1)} %param.20, s32[]{:T(128)S(6)} %select_n.8, pred[4096,32]{1,0:T(8,128)(4,1)S(1)} %iota_compare_fusion), kind=kLoop, calls=%fused_computation | loop fusion | flops 262144 | bytes 1179652 | tf_op jit(solution)/shard_map/jit(_where)/select_n | solution.py:377
  41.1 1.8 %copy.17.taps_ref = bf16[32,64,128]{2,1,0:T(8,128)(2,1)} copy(bf16[32,64,128]{0,2,1:T(8,128)(2,1)S(1)} %bitcast.4) | data formatting | bytes 1048576 | tf_op jit(solution)/shard_map/reshape | solution.py:378
  42.9 13.2 %shard_map.146.h_hbm = f32[32,160,256]{2,1,0:T(8,128)} custom-call(bf16[32,64,128]{2,1,0:T(8,128)(2,1)} %copy.17.taps_ref, bf16[640,64]{1,0:T(8,128)(2,1)} %constant.26.clone.w1_ref, f32[2,160,128]{2,1,0:T(8,128)} %constant.27.clone.tw_ref, bf16[768,256]{1,0:T(8,128)(2,1)} %constant.28.clone.wp_ref.wq_ref), custom_call_target="tpu_custom_call" | custom-call | flops 4000000000 | bytes 8000000 | tf_op jit(solution)/shard_map/pallas_call | solution.py:216
  56.1 12.0 %all-to-all-done.x_ref = bf16[128,32,256]{2,1,0:T(8,128)(2,1)} async-done(((bf16[128,32,256]{2,1,0:T(8,128)(2,1)}), bf16[128,32,256]{2,1,0:T(8,128)(2,1)}, u32[]{:S(2)}, u32[]{:S(2)}) %all-to-all-start) | async-done | bytes 2097184 | tf_op jit(solution)/shard_map/all_to_all | solution.py:385
  68.1 20.9 %shard_map.147 = bf16[8,1024,128]{2,1,0:T(8,128)(2,1)} custom-call(bf16[128,32,256]{2,1,0:T(8,128)(2,1)} %all-to-all-done.x_ref, f32[32,160,256]{2,1,0:T(8,128)} %shard_map.146.h_hbm, bf16[640,256]{1,0:T(8,128)(2,1)} %constant.29.clone.w1_ref, f32[2,160,128]{2,1,0:T(8,128)} %constant.27.clone.tw_ref, bf16[768,256]{1,0:T(8,128)(2,1)} %constant.30.clone.wp_ref, ...), custom_call_target="tpu_custom_call" | custom-call | flops 6000000000 | bytes 10000000 | tf_op jit(solution)/shard_map/pallas_call | solution.py:328
  88.9 32.1 %all_to_all.10.y_ref = bf16[8,1024,128]{2,1,0:T(8,128)(2,1)} all-to-all(bf16[8,1024,128]{2,1,0:T(8,128)(2,1)} %shard_map.147), channel_id=1, replica_groups=mesh['az'=8,'rg'=16] {'az'}, dimensions={0} | all-to-all | bytes 4194304 | tf_op jit(solution)/shard_map/all_to_all | solution.py:388
  121.0 3.7 %shard_map.148 = f32[2,2048,256]{2,1,0:T(8,128)} custom-call(bf16[8,1024,128]{2,1,0:T(8,128)(2,1)} %all_to_all.10.y_ref), custom_call_target="tpu_custom_call" | custom-call | bytes 6000000 | tf_op jit(solution)/shard_map/pallas_call | solution.py:359
Async XLA Ops:
  26.2 12.0 %copy-start = (s32[256]{0:T(256)S(1)}, s32[256]{0:T(256)}, u32[]{:S(2)}) copy-start(s32[256]{0:T(256)} %param.21) | copy-start | bytes 3076
  26.2 41.9 %all-to-all-start = ((bf16[128,32,256]{2,1,0:T(8,128)(2,1)}), bf16[128,32,256]{2,1,0:T(8,128)(2,1)}, u32[]{:S(2)}, u32[]{:S(2)}) async-start(bf16[128,32,256]{2,1,0:T(8,128)(2,1)} %bitcast.5), calls=%async_computation | async-start | bytes 4194304 | tf_op jit(solution)/shard_map/all_to_all | solution.py:385

commit v3 on v2

--- a/solution.py
+++ b/solution.py
@@ -21,6 +21,9 @@
 MOUT = 128
 MFIL = 32
 NBIN = 32
+PIECES = 4
+SIDE = 2
+PITCH = 40
 VMEM = 60 * 1024 * 1024
 GROUPS = (11, 11, 11)
 EARLY = 8
@@ -223,29 +226,41 @@
     )(taps, jnp.asarray(w1), jnp.asarray(twiddle()), jnp.asarray(wp))
 
 
-def focus_kernel(x_ref, h_hbm, w1_ref, tw_ref, wp_ref, wq_ref, w3_ref, out_ref, s_ref, z_ref, h_ref, *scratch):
-    stage1, stage2, stage3, sem = scratch[0:2], scratch[2:4], scratch[4:6], scratch[6]
-    copy = pltpu.make_async_copy(h_hbm, h_ref, sem)
-    copy.start()
+def focus_kernel(x_hbm, h_hbm, w1_hbm, tw_hbm, wp_hbm, wq_hbm, w3_hbm, out_hbm, *scratch):
+    x_ref, h_ref, w1_ref, tw_ref, wp_ref, wq_ref, w3_ref, out_ref, s_ref, z_ref = scratch[:10]
+    stage1, stage2, stage3 = scratch[10:12], scratch[12:14], scratch[14:16]
+    x_sems, t_sems, o_sems = scratch[16:]
+    piece = MSRC // PIECES
+    arriving = []
+    for i in range(PIECES):
+        part = pl.ds(i * piece, piece)
+        arriving.append(pltpu.make_async_copy(x_hbm.at[part], x_ref.at[part], x_sems.at[i]))
+    tables = [(w1_hbm, w1_ref), (tw_hbm, tw_ref), (h_hbm, h_ref), (wp_hbm, wp_ref), (wq_hbm, wq_ref), (w3_hbm, w3_ref)]
+    tables = [pltpu.make_async_copy(src, dst, t_sems.at[i]) for i, (src, dst) in enumerate(tables)]
+    for copy in arriving + tables:
+        copy.start()
 
     def widen(m, _):
         part = x_ref[m].astype(F32)
-        s_ref[pl.ds(pl.multiple_of(m * NBIN, NBIN), NBIN), :] = part[:, :BLK]
-        s_ref[pl.ds(pl.multiple_of((MSRC + m) * NBIN, NBIN), NBIN), :] = part[:, BLK:]
-        return 0
-
-    lax.fori_loop(0, MSRC, widen, 0, unroll=8)
-    copy.wait()
+        s_ref[pl.ds(pl.multiple_of(m * PITCH, 8), NBIN), :] = part[:, :BLK]
+        s_ref[pl.ds(pl.multiple_of((MSRC + m) * PITCH, 8), NBIN), :] = part[:, BLK:]
+        return 0
+
+    for i in range(PIECES):
+        arriving[i].wait()
+        lax.fori_loop(i * piece, (i + 1) * piece, widen, 0, unroll=8)
+    for copy in tables:
+        copy.wait()
 
     def load(b):
-        return s_ref[pl.ds(b, 2 * MSRC, stride=NBIN), :].astype(BF)
+        return s_ref[pl.ds(b, 2 * MSRC, stride=PITCH), :].astype(BF)
 
     def coarse(i, to):
-        both = jnp.concatenate([load(2 * i), load(2 * i + 1)], axis=1)
+        both = jnp.concatenate([load(SIDE * i + u) for u in range(SIDE)], axis=1)
         first = dot(w1_ref[...], both)
         first = first[: 2 * N1] + first[2 * N1 :]
         c, s = tw_ref[0], tw_ref[1]
-        for u in range(2):
+        for u in range(SIDE):
             rows = slice(u * N1, (u + 1) * N1)
             re = first[:N1, u * BLK : (u + 1) * BLK]
             im = first[N1:, u * BLK : (u + 1) * BLK]
@@ -257,19 +272,19 @@
 
     def fine(i, at, to):
         spectrum = dot(wide(at), wp_ref[...])
-        for u in range(2):
+        for u in range(SIDE):
             rows = slice(u * N1, (u + 1) * N1)
             xr = spectrum[rows, :BLK]
             xi = spectrum[rows, BLK:]
-            hr = h_ref[2 * i + u, :, :BLK]
-            hi = h_ref[2 * i + u, :, BLK:]
+            hr = h_ref[SIDE * i + u, :, :BLK]
+            hi = h_ref[SIDE * i + u, :, BLK:]
             to[rows, 0:BLK], to[rows, 2 * BLK : 3 * BLK] = parts(xr * hr - xi * hi)
             to[rows, BLK : 2 * BLK], to[rows, 3 * BLK :] = parts(xr * hi + xi * hr)
 
     def fine_back(at, to):
         back = dot(wide(at), wq_ref[...])
         c, s = tw_ref[0], tw_ref[1]
-        for u in range(2):
+        for u in range(SIDE):
             lanes = slice(u * BLK, (u + 1) * BLK)
             re = back[u * N1 : (u + 1) * N1, :BLK]
             im = back[u * N1 : (u + 1) * N1, BLK:]
@@ -278,10 +293,10 @@
 
     def coarse_back(i, at):
         last = dot(w3_ref[...], jnp.concatenate([at[...], at[: 2 * N1, :]], axis=0))
-        for u in range(2):
-            z_ref[pl.ds(2 * i + u, 2 * MOUT, stride=NBIN), :] = last[:, u * BLK : (u + 1) * BLK]
-
-    pairs = NBIN // 2
+        for u in range(SIDE):
+            z_ref[pl.ds(SIDE * i + u, 2 * MOUT, stride=PITCH), :] = last[:, u * BLK : (u + 1) * BLK]
+
+    pairs = NBIN // SIDE
 
     def step(q, parity, first, last):
         if first <= 3 <= last:
@@ -307,15 +322,27 @@
         step(q, q % 2, q - pairs + 1, 3)
 
     n_az = out_ref.shape[0]
-    rows = MOUT // n_az * NBIN
+    blocks = MOUT // n_az
+
+    def leave(a):
+        return pltpu.make_async_copy(out_ref.at[a], out_hbm.at[a], o_sems.at[a])
 
     def narrow(a, _):
         for part in range(2):
-            o = pl.multiple_of((part * n_az + a) * rows, rows)
-            out_ref[a, part * rows : (part + 1) * rows, :] = z_ref[pl.ds(o, rows), :].astype(BF)
+            for m in range(blocks):
+                o = pl.multiple_of(((part * n_az + a) * blocks + m) * PITCH, 8)
+                row = (part * blocks + m) * NBIN
+                out_ref[a, row : row + NBIN, :] = z_ref[pl.ds(o, NBIN), :].astype(BF)
+        leave(a).start()
         return 0
 
     lax.fori_loop(0, n_az, narrow, 0)
+
+    def left(a, _):
+        leave(a).wait()
+        return 0
+
+    lax.fori_loop(0, n_az, left, 0)
 
 
 def focus(x, spectrum, n_az, n_rg):
@@ -324,49 +351,75 @@
     wp = right_table(angles(np.arange(BLK), np.arange(BLK), BLK), -1.0)
     wq = right_table(angles(np.arange(BLK), np.arange(BLK), BLK), 1.0)
     w3 = left_table(angles(np.arange(MOUT), np.arange(N1), N1), 1.0)
-    vmem = pl.BlockSpec(memory_space=pltpu.VMEM)
+    hbm = pl.BlockSpec(memory_space=pltpu.HBM)
+    out = (n_az, 2 * MOUT // n_az * NBIN, BLK)
+    tables = [(w1, BF), (twiddle(), F32), (wp, BF), (wq, BF), (w3, BF)]
     return pl.pallas_call(
         focus_kernel,
-        out_shape=jax.ShapeDtypeStruct((n_az, 2 * MOUT // n_az * NBIN, BLK), BF),
-        in_specs=[vmem, pl.BlockSpec(memory_space=pl.ANY)] + [vmem] * 5,
-        out_specs=vmem,
+        out_shape=jax.ShapeDtypeStruct(out, BF),
+        in_specs=[hbm] * 7,
+        out_specs=hbm,
         scratch_shapes=[
-            pltpu.VMEM((2 * MSRC * NBIN, BLK), F32),
-            pltpu.VMEM((2 * MOUT * NBIN, BLK), F32),
-            pltpu.VMEM((NBIN, N1, 2 * BLK), F32),
-            *[pltpu.VMEM((2 * N1, 4 * BLK), BF)] * 4,
-            *[pltpu.VMEM((4 * N1, 2 * BLK), BF)] * 2,
-            pltpu.SemaphoreType.DMA(()),
+            pltpu.VMEM(x.shape, BF),
+            pltpu.VMEM(spectrum.shape, F32),
+            *[pltpu.VMEM(table.shape, kind) for table, kind in tables],
+            pltpu.VMEM(out, BF),
+            pltpu.VMEM((2 * MSRC * PITCH, BLK), F32),
+            pltpu.VMEM((2 * MOUT * PITCH, BLK), F32),
+            *[pltpu.VMEM((SIDE * N1, 4 * BLK), BF)] * 4,
+            *[pltpu.VMEM((4 * N1, SIDE * BLK), BF)] * 2,
+            pltpu.SemaphoreType.DMA((PIECES,)),
+            pltpu.SemaphoreType.DMA((6,)),
+            pltpu.SemaphoreType.DMA((n_az,)),
         ],
         compiler_params=pltpu.CompilerParams(vmem_limit_bytes=VMEM),
         cost_estimate=pl.CostEstimate(flops=6_000_000_000, bytes_accessed=10_000_000, transcendentals=0),
-    )(x, spectrum, jnp.asarray(w1), jnp.asarray(twiddle()), jnp.asarray(wp), jnp.asarray(wq), jnp.asarray(w3))
-
-
-def turn_kernel(y_ref, out_ref):
+    )(x, spectrum, *[jnp.asarray(table) for table, _ in tables])
+
+
+def turn_kernel(y_hbm, out_hbm, y_ref, out_ref, in_sems, out_sems):
     n_az, rows, _ = y_ref.shape
+    piece = rows // PIECES
+    arriving = []
+    for i in range(PIECES):
+        part = pl.ds(i * piece, piece)
+        arriving.append(pltpu.make_async_copy(y_hbm.at[:, part, :], y_ref.at[:, part, :], in_sems.at[i]))
+        arriving[-1].start()
     row_of = lax.broadcasted_iota(jnp.int32, (BLK, BLK), 0)
     col_of = lax.broadcasted_iota(jnp.int32, (BLK, BLK), 1)
     unit = jnp.where(row_of == col_of, 1.0, 0.0).astype(BF)
-    for i in range(rows // NBIN):
-        part = y_ref[:, i * NBIN : (i + 1) * NBIN, :].reshape(n_az * NBIN, BLK)
-        out_ref[0, i * BLK : (i + 1) * BLK, :] = lax.dot_general(unit, part, NT, preferred_element_type=F32)
+    leaving = []
+    for i in range(PIECES):
+        arriving[i].wait()
+        for k in range(i * piece // NBIN, (i + 1) * piece // NBIN):
+            part = y_ref[:, k * NBIN : (k + 1) * NBIN, :].reshape(n_az * NBIN, BLK)
+            out_ref[k * BLK : (k + 1) * BLK, :] = lax.dot_general(unit, part, NT, preferred_element_type=F32)
+        done = pl.ds(i * piece // NBIN * BLK, piece // NBIN * BLK)
+        leaving.append(pltpu.make_async_copy(out_ref.at[done, :], out_hbm.at[done, :], out_sems.at[i]))
+        leaving[-1].start()
+    for copy in leaving:
+        copy.wait()
 
 
 def turn(y):
     n_az, rows, _ = y.shape
-    steps = 2
-    return pl.pallas_call(
+    out = (rows // NBIN * BLK, n_az * NBIN)
+    hbm = pl.BlockSpec(memory_space=pltpu.HBM)
+    image = pl.pallas_call(
         turn_kernel,
-        grid=(steps,),
-        out_shape=jax.ShapeDtypeStruct((2, rows // NBIN // 2 * BLK, n_az * NBIN), F32),
-        in_specs=[pl.BlockSpec((n_az, rows // steps, BLK), lambda g: (0, g, 0))],
-        out_specs=pl.BlockSpec(
-            (1, rows // NBIN // steps * BLK, n_az * NBIN), lambda g: (g // (steps // 2), g % (steps // 2), 0)
-        ),
+        out_shape=jax.ShapeDtypeStruct(out, F32),
+        in_specs=[hbm],
+        out_specs=hbm,
+        scratch_shapes=[
+            pltpu.VMEM(y.shape, BF),
+            pltpu.VMEM(out, F32),
+            pltpu.SemaphoreType.DMA((PIECES,)),
+            pltpu.SemaphoreType.DMA((PIECES,)),
+        ],
         compiler_params=pltpu.CompilerParams(vmem_limit_bytes=VMEM),
         cost_estimate=pl.CostEstimate(flops=0, bytes_accessed=6_000_000, transcendentals=0),
     )(y)
+    return image.reshape(2, out[0] // 2, out[1])
 
 
 def own_taps(az_filter, az_lengths):

time: 125 us -> 121 us (0.968)
  Pallas kernels: 63.9 us -> 59.2 us
    pallas_call x2, Pallas kernels: 24.5 us -> 19.9 us  [the longest x1 16.5 us: focus(): pl.pallas_call(focus_kernel, out_shape=jax.ShapeDtypeStruct(out, BF), in_...]
where the time goes in v3:
time: 121 us; the launch traced here: 120 us
  Pallas kernels  59.2 us (49%)
  blocking collectives  32.1 us (27%)
  starting transfers between devices  12 us (10%)
  waiting for transfers between devices  12 us (10%)
  other arithmetic  2.85 us (2%)
  local copies, waits for them, and re-layouts  1.88 us (2%)
    all_to_all x1, blocking collectives, per_device(): y = lax.all_to_all(y, 'az', 0, 0, tiled=True)  32.1 us
    pallas_call x1, Pallas kernels, compress(): pl.pallas_call(compress_kernel, out_shape=jax.ShapeDtypeStruct((NBLK * BL...  26.2 us
    pallas_call x1, Pallas kernels, focus(): pl.pallas_call(focus_kernel, out_shape=jax.ShapeDtypeStruct(out, BF), in_...  16.5 us
    pallas_call x1, Pallas kernels, filter_spectrum(): pl.pallas_call(filter_kernel, out_shape=jax.ShapeDtypeStruct((NBIN, N1, 2...  13.2 us
    all_to_all x1, waiting for transfers between devices, per_device(): x = lax.all_to_all(moved, ('rg', 'az'), 0, 0, tiled=True)  12 us
    all_to_all x1, starting transfers between devices, per_device(): x = lax.all_to_all(moved, ('rg', 'az'), 0, 0, tiled=True)  12 us
    pallas_call x1, Pallas kernels, turn(): pl.pallas_call(turn_kernel, out_shape=jax.ShapeDtypeStruct(out, F32), in_...  3.42 us
    select_n x1, other arithmetic, own_taps(): taps = jnp.where(kept[None], taps, jnp.zeros((), BF))  2.5 us
  transfers between devices with their start and end apart: 1, of which 1 were waited for; matrix products, arithmetic and copies ran while one was open for 4% of the time, Pallas kernels for 11%

profile of v3, /device:TPU:1, one launch (start us, length us, event | category | flops | bytes accessed | tf_op | source)
XLA Modules:
  0.0 120.2 jit_solution(7660548370147918881)
XLA Ops:
  0.0 26.2 %shard_map.145 = bf16[4096,256]{1,0:T(8,128)(2,1)} custom-call(s32[32]{0:T(128)} %off_hbm.1, s32[32]{0:T(128)} %wid_hbm.1, bf16[2,4096]{1,0:T(2,128)(2,1)} %filt_ref.1, bf16[32,32]{1,0:T(8,128)(2,1)} %coef_ref.1, bf16[2,128,8320]{2,1,0:T(8,128)(2,1)} %raw_hbm.1), custom_call_target="tpu_custom_call" | custom-call | flops 18300000256 | bytes 8000000 | tf_op jit(solution)/shard_map/pallas_call | solution.py:132
  26.2 0.0 copy-start
  26.2 12.0 %all-to-all-start = ((bf16[128,32,256]{2,1,0:T(8,128)(2,1)}), bf16[128,32,256]{2,1,0:T(8,128)(2,1)}, u32[]{:S(2)}, u32[]{:S(2)}) async-start(bf16[128,32,256]{2,1,0:T(8,128)(2,1)} %bitcast.6), calls=%async_computation | async-start | bytes 4194304 | tf_op jit(solution)/shard_map/all_to_all | solution.py:438
  38.2 0.0 copy-done
  38.2 0.1 dynamic_slice.6
  38.3 0.3 iota_compare_fusion
  38.6 2.5 %dynamic-slice_select_fusion = bf16[2,4096,32]{2,1,0:T(8,128)(2,1)S(1)} fusion(bf16[2,4096,256]{2,1,0:T(8,128)(2,1)} %param.20, s32[]{:T(128)S(6)} %select_n.8, pred[4096,32]{1,0:T(8,128)(4,1)S(1)} %iota_compare_fusion), kind=kLoop, calls=%fused_computation | loop fusion | flops 262144 | bytes 1179652 | tf_op jit(solution)/shard_map/jit(_where)/select_n | solution.py:430
  41.1 1.8 %copy.17.taps_ref = bf16[32,64,128]{2,1,0:T(8,128)(2,1)} copy(bf16[32,64,128]{0,2,1:T(8,128)(2,1)S(1)} %bitcast.5) | data formatting | bytes 1048576 | tf_op jit(solution)/shard_map/reshape | solution.py:431
  42.9 13.2 %shard_map.146.h_hbm = f32[32,160,256]{2,1,0:T(8,128)} custom-call(bf16[32,64,128]{2,1,0:T(8,128)(2,1)} %copy.17.taps_ref, bf16[640,64]{1,0:T(8,128)(2,1)} %constant.26.clone.w1_ref, f32[2,160,128]{2,1,0:T(8,128)} %constant.27.clone.tw_ref.tw_hbm, bf16[768,256]{1,0:T(8,128)(2,1)} %constant.28.clone.wp_ref.wq_hbm), custom_call_target="tpu_custom_call" | custom-call | flops 4000000000 | bytes 8000000 | tf_op jit(solution)/shard_map/pallas_call | solution.py:219
  56.1 12.0 %all-to-all-done.x_hbm = bf16[128,32,256]{2,1,0:T(8,128)(2,1)} async-done(((bf16[128,32,256]{2,1,0:T(8,128)(2,1)}), bf16[128,32,256]{2,1,0:T(8,128)(2,1)}, u32[]{:S(2)}, u32[]{:S(2)}) %all-to-all-start) | async-done | bytes 2097184 | tf_op jit(solution)/shard_map/all_to_all | solution.py:438
  68.1 16.5 %shard_map.147 = bf16[8,1024,128]{2,1,0:T(8,128)(2,1)} custom-call(bf16[128,32,256]{2,1,0:T(8,128)(2,1)} %all-to-all-done.x_hbm, f32[32,160,256]{2,1,0:T(8,128)} %shard_map.146.h_hbm, bf16[640,256]{1,0:T(8,128)(2,1)} %constant.29.clone.w1_hbm, f32[2,160,128]{2,1,0:T(8,128)} %constant.27.clone.tw_ref.tw_hbm, bf16[768,256]{1,0:T(8,128)(2,1)} %constant.30.clone.wp_hbm, ...), custom_call_target="tpu_custom_call" | custom-call | flops 6000000000 | bytes 10000000 | tf_op jit(solution)/shard_map/pallas_call | solution.py:357
  84.6 32.1 %all_to_all.10.y_hbm = bf16[8,1024,128]{2,1,0:T(8,128)(2,1)} all-to-all(bf16[8,1024,128]{2,1,0:T(8,128)(2,1)} %shard_map.147), channel_id=1, replica_groups=mesh['az'=8,'rg'=16] {'az'}, dimensions={0} | all-to-all | bytes 4194304 | tf_op jit(solution)/shard_map/all_to_all | solution.py:441
  116.6 3.4 %shard_map.148 = f32[4096,256]{1,0:T(8,128)} custom-call(bf16[8,1024,128]{2,1,0:T(8,128)(2,1)} %all_to_all.10.y_hbm), custom_call_target="tpu_custom_call" | custom-call | bytes 6000000 | tf_op jit(solution)/shard_map/pallas_call | solution.py:408
Async XLA Ops:
  26.2 12.0 %copy-start = (s32[256]{0:T(256)S(1)}, s32[256]{0:T(256)}, u32[]{:S(2)}) copy-start(s32[256]{0:T(256)} %param.21) | copy-start | bytes 3076
  26.2 41.9 %all-to-all-start = ((bf16[128,32,256]{2,1,0:T(8,128)(2,1)}), bf16[128,32,256]{2,1,0:T(8,128)(2,1)}, u32[]{:S(2)}, u32[]{:S(2)}) async-start(bf16[128,32,256]{2,1,0:T(8,128)(2,1)} %bitcast.6), calls=%async_computation | async-start | bytes 4194304 | tf_op jit(solution)/shard_map/all_to_all | solution.py:438

commit v4 on v3

--- a/solution.py
+++ b/solution.py
@@ -21,8 +21,9 @@
 MOUT = 128
 MFIL = 32
 NBIN = 32
-PIECES = 4
-SIDE = 2
+PIECES = 8
+TURNS = 4
+SIDE = 4
 PITCH = 40
 VMEM = 60 * 1024 * 1024
 GROUPS = (11, 11, 11)
@@ -113,7 +114,7 @@
             acc = acc + dot(both, g_ref[j * 2 * BLK : (j + 1) * 2 * BLK, :])
             if done == 0 and j + EARLY < NOUT:
                 table(j + EARLY)
-            if j % 2 == 1 and moved < done - 1:
+            if j % 3 == 2 and moved < done - 1:
                 migrate(moved)
                 moved += 1
         out = acc.astype(BF)
@@ -264,14 +265,14 @@
             rows = slice(u * N1, (u + 1) * N1)
             re = first[:N1, u * BLK : (u + 1) * BLK]
             im = first[N1:, u * BLK : (u + 1) * BLK]
-            to[rows, 0:BLK], to[rows, 2 * BLK : 3 * BLK] = parts(re * c + im * s)
-            to[rows, BLK : 2 * BLK], to[rows, 3 * BLK :] = parts(im * c - re * s)
+            to[rows, 0:BLK] = (re * c + im * s).astype(BF)
+            to[rows, BLK:] = (im * c - re * s).astype(BF)
 
     def wide(at):
         return jnp.concatenate([at[...], at[:, : 2 * BLK]], axis=1)
 
     def fine(i, at, to):
-        spectrum = dot(wide(at), wp_ref[...])
+        spectrum = dot(jnp.concatenate([at[...], at[...]], axis=1), wp_ref[...])
         for u in range(SIDE):
             rows = slice(u * N1, (u + 1) * N1)
             xr = spectrum[rows, :BLK]
@@ -348,7 +349,8 @@
 def focus(x, spectrum, n_az, n_rg):
     order = source_order(n_az, n_rg)
     w1 = stacked_table(angles(np.arange(N1), order, N1), -1.0)
-    wp = right_table(angles(np.arange(BLK), np.arange(BLK), BLK), -1.0)
+    hi, lo = complex_table(angles(np.arange(BLK), np.arange(BLK), BLK), -1.0)
+    wp = np.concatenate([hi.T, lo.T], axis=0)
     wq = right_table(angles(np.arange(BLK), np.arange(BLK), BLK), 1.0)
     w3 = left_table(angles(np.arange(MOUT), np.arange(N1), N1), 1.0)
     hbm = pl.BlockSpec(memory_space=pltpu.HBM)
@@ -366,7 +368,8 @@
             pltpu.VMEM(out, BF),
             pltpu.VMEM((2 * MSRC * PITCH, BLK), F32),
             pltpu.VMEM((2 * MOUT * PITCH, BLK), F32),
-            *[pltpu.VMEM((SIDE * N1, 4 * BLK), BF)] * 4,
+            *[pltpu.VMEM((SIDE * N1, 2 * BLK), BF)] * 2,
+            *[pltpu.VMEM((SIDE * N1, 4 * BLK), BF)] * 2,
             *[pltpu.VMEM((4 * N1, SIDE * BLK), BF)] * 2,
             pltpu.SemaphoreType.DMA((PIECES,)),
             pltpu.SemaphoreType.DMA((6,)),
@@ -379,9 +382,9 @@
 
 def turn_kernel(y_hbm, out_hbm, y_ref, out_ref, in_sems, out_sems):
     n_az, rows, _ = y_ref.shape
-    piece = rows // PIECES
+    piece = rows // TURNS
     arriving = []
-    for i in range(PIECES):
+    for i in range(TURNS):
         part = pl.ds(i * piece, piece)
         arriving.append(pltpu.make_async_copy(y_hbm.at[:, part, :], y_ref.at[:, part, :], in_sems.at[i]))
         arriving[-1].start()
@@ -389,7 +392,7 @@
     col_of = lax.broadcasted_iota(jnp.int32, (BLK, BLK), 1)
     unit = jnp.where(row_of == col_of, 1.0, 0.0).astype(BF)
     leaving = []
-    for i in range(PIECES):
+    for i in range(TURNS):
         arriving[i].wait()
         for k in range(i * piece // NBIN, (i + 1) * piece // NBIN):
             part = y_ref[:, k * NBIN : (k + 1) * NBIN, :].reshape(n_az * NBIN, BLK)
@@ -413,8 +416,8 @@
         scratch_shapes=[
             pltpu.VMEM(y.shape, BF),
             pltpu.VMEM(out, F32),
-            pltpu.SemaphoreType.DMA((PIECES,)),
-            pltpu.SemaphoreType.DMA((PIECES,)),
+            pltpu.SemaphoreType.DMA((TURNS,)),
+            pltpu.SemaphoreType.DMA((TURNS,)),
         ],
         compiler_params=pltpu.CompilerParams(vmem_limit_bytes=VMEM),
         cost_estimate=pl.CostEstimate(flops=0, bytes_accessed=6_000_000, transcendentals=0),

time: 121 us -> 118 us (0.975)
  Pallas kernels: 59.2 us -> 56.9 us
    pallas_call x1, Pallas kernels: 16.5 us -> 14.5 us  [focus(): pl.pallas_call(focus_kernel, out_shape=jax.ShapeDtypeStruct(out, BF), in_...]
where the time goes in v4:
time: 118 us
  Pallas kernels  56.9 us (48%)
  blocking collectives  32.1 us (27%)
  starting transfers between devices  12 us (10%)
  waiting for transfers between devices  12 us (10%)
  other arithmetic  2.85 us (2%)
  local copies, waits for them, and re-layouts  1.88 us (2%)
    all_to_all x1, blocking collectives, per_device(): y = lax.all_to_all(y, 'az', 0, 0, tiled=True)  32.1 us
    pallas_call x1, Pallas kernels, compress(): pl.pallas_call(compress_kernel, out_shape=jax.ShapeDtypeStruct((NBLK * BL...  25.8 us
    pallas_call x1, Pallas kernels, focus(): pl.pallas_call(focus_kernel, out_shape=jax.ShapeDtypeStruct(out, BF), in_...  14.5 us
    pallas_call x1, Pallas kernels, filter_spectrum(): pl.pallas_call(filter_kernel, out_shape=jax.ShapeDtypeStruct((NBIN, N1, 2...  13.2 us
    all_to_all x1, waiting for transfers between devices, per_device(): x = lax.all_to_all(moved, ('rg', 'az'), 0, 0, tiled=True)  12 us
    all_to_all x1, starting transfers between devices, per_device(): x = lax.all_to_all(moved, ('rg', 'az'), 0, 0, tiled=True)  12 us
    pallas_call x1, Pallas kernels, turn(): pl.pallas_call(turn_kernel, out_shape=jax.ShapeDtypeStruct(out, F32), in_...  3.41 us
    select_n x1, other arithmetic, own_taps(): taps = jnp.where(kept[None], taps, jnp.zeros((), BF))  2.5 us
  transfers between devices with their start and end apart: 1, of which 1 were waited for; matrix products, arithmetic and copies ran while one was open for 4% of the time, Pallas kernels for 11%

profile of v4, /device:TPU:1, one launch (start us, length us, event | category | flops | bytes accessed | tf_op | source)
XLA Modules:
  0.0 117.8 jit_solution(3254072743817645431)
XLA Ops:
  0.0 25.8 %shard_map.145 = bf16[4096,256]{1,0:T(8,128)(2,1)} custom-call(s32[32]{0:T(128)} %off_hbm.1, s32[32]{0:T(128)} %wid_hbm.1, bf16[2,4096]{1,0:T(2,128)(2,1)} %filt_ref.1, bf16[32,32]{1,0:T(8,128)(2,1)} %coef_ref.1, bf16[2,128,8320]{2,1,0:T(8,128)(2,1)} %raw_hbm.1), custom_call_target="tpu_custom_call" | custom-call | flops 18300000256 | bytes 8000000 | tf_op jit(solution)/shard_map/pallas_call | solution.py:133
  25.8 0.0 copy-start
  25.9 12.0 %all-to-all-start = ((bf16[128,32,256]{2,1,0:T(8,128)(2,1)}), bf16[128,32,256]{2,1,0:T(8,128)(2,1)}, u32[]{:S(2)}, u32[]{:S(2)}) async-start(bf16[128,32,256]{2,1,0:T(8,128)(2,1)} %bitcast.6), calls=%async_computation | async-start | bytes 4194304 | tf_op jit(solution)/shard_map/all_to_all | solution.py:441
  37.8 0.0 copy-done
  37.8 0.1 dynamic_slice.6
  37.9 0.3 iota_compare_fusion
  38.3 2.5 %dynamic-slice_select_fusion = bf16[2,4096,32]{2,1,0:T(8,128)(2,1)S(1)} fusion(bf16[2,4096,256]{2,1,0:T(8,128)(2,1)} %param.20, s32[]{:T(128)S(6)} %select_n.8, pred[4096,32]{1,0:T(8,128)(4,1)S(1)} %iota_compare_fusion), kind=kLoop, calls=%fused_computation | loop fusion | flops 262144 | bytes 1179652 | tf_op jit(solution)/shard_map/jit(_where)/select_n | solution.py:433
  40.8 1.8 %copy.17.taps_ref = bf16[32,64,128]{2,1,0:T(8,128)(2,1)} copy(bf16[32,64,128]{0,2,1:T(8,128)(2,1)S(1)} %bitcast.5) | data formatting | bytes 1048576 | tf_op jit(solution)/shard_map/reshape | solution.py:434
  42.6 13.2 %shard_map.146.h_hbm = f32[32,160,256]{2,1,0:T(8,128)} custom-call(bf16[32,64,128]{2,1,0:T(8,128)(2,1)} %copy.17.taps_ref, bf16[640,64]{1,0:T(8,128)(2,1)} %constant.26.clone.w1_ref, f32[2,160,128]{2,1,0:T(8,128)} %constant.27.clone.tw_ref.tw_hbm, bf16[768,256]{1,0:T(8,128)(2,1)} %constant.28.clone.wp_ref.wq_hbm), custom_call_target="tpu_custom_call" | custom-call | flops 4000000000 | bytes 8000000 | tf_op jit(solution)/shard_map/pallas_call | solution.py:220
  55.7 12.0 %all-to-all-done.x_hbm = bf16[128,32,256]{2,1,0:T(8,128)(2,1)} async-done(((bf16[128,32,256]{2,1,0:T(8,128)(2,1)}), bf16[128,32,256]{2,1,0:T(8,128)(2,1)}, u32[]{:S(2)}, u32[]{:S(2)}) %all-to-all-start) | async-done | bytes 2097184 | tf_op jit(solution)/shard_map/all_to_all | solution.py:441
  67.7 14.5 %shard_map.147 = bf16[8,1024,128]{2,1,0:T(8,128)(2,1)} custom-call(bf16[128,32,256]{2,1,0:T(8,128)(2,1)} %all-to-all-done.x_hbm, f32[32,160,256]{2,1,0:T(8,128)} %shard_map.146.h_hbm, bf16[640,256]{1,0:T(8,128)(2,1)} %constant.29.clone.w1_hbm, f32[2,160,128]{2,1,0:T(8,128)} %constant.27.clone.tw_ref.tw_hbm, bf16[512,256]{1,0:T(8,128)(2,1)} %constant.30.clone.wp_hbm, ...), custom_call_target="tpu_custom_call" | custom-call | flops 6000000000 | bytes 10000000 | tf_op jit(solution)/shard_map/pallas_call | solution.py:359
  82.2 32.1 %all_to_all.10.y_hbm = bf16[8,1024,128]{2,1,0:T(8,128)(2,1)} all-to-all(bf16[8,1024,128]{2,1,0:T(8,128)(2,1)} %shard_map.147), channel_id=1, replica_groups=mesh['az'=8,'rg'=16] {'az'}, dimensions={0} | all-to-all | bytes 4194304 | tf_op jit(solution)/shard_map/all_to_all | solution.py:444
  114.3 3.4 %shard_map.148 = f32[4096,256]{1,0:T(8,128)} custom-call(bf16[8,1024,128]{2,1,0:T(8,128)(2,1)} %all_to_all.10.y_hbm), custom_call_target="tpu_custom_call" | custom-call | bytes 6000000 | tf_op jit(solution)/shard_map/pallas_call | solution.py:411
Async XLA Ops:
  25.8 12.0 %copy-start = (s32[256]{0:T(256)S(1)}, s32[256]{0:T(256)}, u32[]{:S(2)}) copy-start(s32[256]{0:T(256)} %param.21) | copy-start | bytes 3076
  25.9 41.9 %all-to-all-start = ((bf16[128,32,256]{2,1,0:T(8,128)(2,1)}), bf16[128,32,256]{2,1,0:T(8,128)(2,1)}, u32[]{:S(2)}, u32[]{:S(2)}) async-start(bf16[128,32,256]{2,1,0:T(8,128)(2,1)} %bitcast.6), calls=%async_computation | async-start | bytes 4194304 | tf_op jit(solution)/shard_map/all_to_all | solution.py:441

commit v5 on v4

--- a/solution.py
+++ b/solution.py
@@ -23,7 +23,7 @@
 NBIN = 32
 PIECES = 8
 TURNS = 4
-SIDE = 4
+SIDE = 8
 PITCH = 40
 VMEM = 60 * 1024 * 1024
 GROUPS = (11, 11, 11)
@@ -36,7 +36,7 @@
 
 
 def compress_kernel(
-    off_hbm, wid_hbm, filt_ref, coef_ref, raw_hbm, out_ref, x_ref, g_ref, c_ref, f_ref, r_ref, w_ref, off_ref, wid_ref, sems, small
+    off_hbm, wid_hbm, filt_ref, coef_ref, raw_hbm, out_hbm, out_ref, x_ref, g_ref, c_ref, f_ref, r_ref, w_ref, off_ref, wid_ref, sems, small, outs
 ):
     def block_copy(s):
         o = pl.multiple_of(s * BLK, BLK)
@@ -123,8 +123,15 @@
             c_ref[done + b, 0:BLK, :] = part[:, :BLK]
             c_ref[done + b, BLK:, :] = part[:, BLK:]
         done += count
+    early = pl.ds(0, moved * BLK)
+    late = pl.ds(moved * BLK, (NBLK - moved) * BLK)
+    sending = [pltpu.make_async_copy(out_ref.at[part, :], out_hbm.at[part, :], outs.at[i]) for i, part in enumerate((early, late))]
+    sending[0].start()
     for b in range(moved, NBLK):
         migrate(b)
+    sending[1].start()
+    for copy in sending:
+        copy.wait()
 
 
 def compress(raw, range_filter, offsets, widths, coefs):
@@ -134,8 +141,9 @@
         compress_kernel,
         out_shape=jax.ShapeDtypeStruct((NBLK * BLK, 2 * BLK), BF),
         in_specs=[hbm, hbm, vmem, vmem, hbm],
-        out_specs=vmem,
+        out_specs=pl.BlockSpec(memory_space=pltpu.HBM),
         scratch_shapes=[
+            pltpu.VMEM((NBLK * BLK, 2 * BLK), BF),
             pltpu.VMEM((2, NSAMP * BLK, BLK), BF),
             pltpu.VMEM((NOUT * 2 * BLK, 2 * BLK), BF),
             pltpu.VMEM((NOUT, 2 * BLK, BLK), BF),
@@ -145,6 +153,7 @@
             pltpu.SMEM((NBLK,), jnp.int32),
             pltpu.SMEM((NBLK,), jnp.int32),
             pltpu.SemaphoreType.DMA((NSAMP,)),
+            pltpu.SemaphoreType.DMA((2,)),
             pltpu.SemaphoreType.DMA((2,)),
         ],
         compiler_params=pltpu.CompilerParams(vmem_limit_bytes=VMEM),

time: 118 us -> 117 us (level)
  no operation moved by 1% of the time
where the time goes in v5:
time: 117 us
  Pallas kernels  56 us (48%)
  blocking collectives  32.1 us (27%)
  starting transfers between devices  12 us (10%)
  waiting for transfers between devices  12 us (10%)
  other arithmetic  2.85 us (2%)
  local copies, waits for them, and re-layouts  1.88 us (2%)
    all_to_all x1, blocking collectives, per_device(): y = lax.all_to_all(y, 'az', 0, 0, tiled=True)  32.1 us
    pallas_call x1, Pallas kernels, compress(): pl.pallas_call(compress_kernel, out_shape=jax.ShapeDtypeStruct((NBLK * BL...  25.4 us
    pallas_call x1, Pallas kernels, focus(): pl.pallas_call(focus_kernel, out_shape=jax.ShapeDtypeStruct(out, BF), in_...  14 us
    pallas_call x1, Pallas kernels, filter_spectrum(): pl.pallas_call(filter_kernel, out_shape=jax.ShapeDtypeStruct((NBIN, N1, 2...  13.2 us
    all_to_all x1, waiting for transfers between devices, per_device(): x = lax.all_to_all(moved, ('rg', 'az'), 0, 0, tiled=True)  12 us
    all_to_all x1, starting transfers between devices, per_device(): x = lax.all_to_all(moved, ('rg', 'az'), 0, 0, tiled=True)  12 us
    pallas_call x1, Pallas kernels, turn(): pl.pallas_call(turn_kernel, out_shape=jax.ShapeDtypeStruct(out, F32), in_...  3.42 us
    select_n x1, other arithmetic, own_taps(): taps = jnp.where(kept[None], taps, jnp.zeros((), BF))  2.5 us
  transfers between devices with their start and end apart: 1, of which 1 were waited for; matrix products, arithmetic and copies ran while one was open for 4% of the time, Pallas kernels for 11%

profile of v5, /device:TPU:1, one launch (start us, length us, event | category | flops | bytes accessed | tf_op | source)
XLA Modules:
  0.0 116.9 jit_solution(9097220422480691644)
XLA Ops:
  0.0 25.4 %shard_map.145 = bf16[4096,256]{1,0:T(8,128)(2,1)} custom-call(s32[32]{0:T(128)} %off_hbm.1, s32[32]{0:T(128)} %wid_hbm.1, bf16[2,4096]{1,0:T(2,128)(2,1)} %filt_ref.1, bf16[32,32]{1,0:T(8,128)(2,1)} %coef_ref.1, bf16[2,128,8320]{2,1,0:T(8,128)(2,1)} %raw_hbm.1), custom_call_target="tpu_custom_call" | custom-call | flops 18300000256 | bytes 8000000 | tf_op jit(solution)/shard_map/pallas_call | solution.py:140
  25.4 0.0 copy-start
  25.4 12.0 %all-to-all-start = ((bf16[128,32,256]{2,1,0:T(8,128)(2,1)}), bf16[128,32,256]{2,1,0:T(8,128)(2,1)}, u32[]{:S(2)}, u32[]{:S(2)}) async-start(bf16[128,32,256]{2,1,0:T(8,128)(2,1)} %bitcast.6), calls=%async_computation | async-start | bytes 4194304 | tf_op jit(solution)/shard_map/all_to_all | solution.py:450
  37.4 0.0 copy-done
  37.4 0.1 dynamic_slice.6
  37.5 0.3 iota_compare_fusion
  37.8 2.5 %dynamic-slice_select_fusion = bf16[2,4096,32]{2,1,0:T(8,128)(2,1)S(1)} fusion(bf16[2,4096,256]{2,1,0:T(8,128)(2,1)} %param.20, s32[]{:T(128)S(6)} %select_n.8, pred[4096,32]{1,0:T(8,128)(4,1)S(1)} %iota_compare_fusion), kind=kLoop, calls=%fused_computation | loop fusion | flops 262144 | bytes 1179652 | tf_op jit(solution)/shard_map/jit(_where)/select_n | solution.py:442
  40.3 1.8 %copy.17.taps_ref = bf16[32,64,128]{2,1,0:T(8,128)(2,1)} copy(bf16[32,64,128]{0,2,1:T(8,128)(2,1)S(1)} %bitcast.5) | data formatting | bytes 1048576 | tf_op jit(solution)/shard_map/reshape | solution.py:443
  42.1 13.2 %shard_map.146.h_hbm = f32[32,160,256]{2,1,0:T(8,128)} custom-call(bf16[32,64,128]{2,1,0:T(8,128)(2,1)} %copy.17.taps_ref, bf16[640,64]{1,0:T(8,128)(2,1)} %constant.26.clone.w1_ref, f32[2,160,128]{2,1,0:T(8,128)} %constant.27.clone.tw_ref.tw_hbm, bf16[768,256]{1,0:T(8,128)(2,1)} %constant.28.clone.wp_ref.wq_hbm), custom_call_target="tpu_custom_call" | custom-call | flops 4000000000 | bytes 8000000 | tf_op jit(solution)/shard_map/pallas_call | solution.py:229
  55.3 12.0 %all-to-all-done.x_hbm = bf16[128,32,256]{2,1,0:T(8,128)(2,1)} async-done(((bf16[128,32,256]{2,1,0:T(8,128)(2,1)}), bf16[128,32,256]{2,1,0:T(8,128)(2,1)}, u32[]{:S(2)}, u32[]{:S(2)}) %all-to-all-start) | async-done | bytes 2097184 | tf_op jit(solution)/shard_map/all_to_all | solution.py:450
  67.3 14.0 %shard_map.147 = bf16[8,1024,128]{2,1,0:T(8,128)(2,1)} custom-call(bf16[128,32,256]{2,1,0:T(8,128)(2,1)} %all-to-all-done.x_hbm, f32[32,160,256]{2,1,0:T(8,128)} %shard_map.146.h_hbm, bf16[640,256]{1,0:T(8,128)(2,1)} %constant.29.clone.w1_hbm, f32[2,160,128]{2,1,0:T(8,128)} %constant.27.clone.tw_ref.tw_hbm, bf16[512,256]{1,0:T(8,128)(2,1)} %constant.30.clone.wp_hbm, ...), custom_call_target="tpu_custom_call" | custom-call | flops 6000000000 | bytes 10000000 | tf_op jit(solution)/shard_map/pallas_call | solution.py:368
  81.3 32.1 %all_to_all.10.y_hbm = bf16[8,1024,128]{2,1,0:T(8,128)(2,1)} all-to-all(bf16[8,1024,128]{2,1,0:T(8,128)(2,1)} %shard_map.147), channel_id=1, replica_groups=mesh['az'=8,'rg'=16] {'az'}, dimensions={0} | all-to-all | bytes 4194304 | tf_op jit(solution)/shard_map/all_to_all | solution.py:453
  113.4 3.4 %shard_map.148 = f32[4096,256]{1,0:T(8,128)} custom-call(bf16[8,1024,128]{2,1,0:T(8,128)(2,1)} %all_to_all.10.y_hbm), custom_call_target="tpu_custom_call" | custom-call | bytes 6000000 | tf_op jit(solution)/shard_map/pallas_call | solution.py:420
Async XLA Ops:
  25.4 12.0 %copy-start = (s32[256]{0:T(256)S(1)}, s32[256]{0:T(256)}, u32[]{:S(2)}) copy-start(s32[256]{0:T(256)} %param.21) | copy-start | bytes 3076
  25.4 41.9 %all-to-all-start = ((bf16[128,32,256]{2,1,0:T(8,128)(2,1)}), bf16[128,32,256]{2,1,0:T(8,128)(2,1)}, u32[]{:S(2)}, u32[]{:S(2)}) async-start(bf16[128,32,256]{2,1,0:T(8,128)(2,1)} %bitcast.6), calls=%async_computation | async-start | bytes 4194304 | tf_op jit(solution)/shard_map/all_to_all | solution.py:450
